TPU v7x, 256 devices: a whole 4x4x8 slice. The times are simulated.
256 devices in a mesh: pa: 16 (over x_lo, y, core), af: 16 (over z, x_hi).
Axes of the slice: x: 4 (x_hi: 2, x_lo: 2; x = x_hi * 2 + x_lo), y: 4, z: 8, core: 2. Of those that a mesh axis runs over, the one named last changes fastest.
Arguments:
- spectra: bfloat16 [2, 57600, 2048], P(None, 'af', 'pa'), may hold values from -64 to 64
- tilt_min: int32 [2048], replicated, may hold values from -70 to -46
- tilt_max: int32 [2048], replicated, may hold values from 46 to 70
- tilt_axis: int32 [2048], replicated, may hold values from 0 to 1
Outputs:
- correlation: float32 [2048, 1152], P(('pa', 'af'))
All inputs are finite; a program needn't handle non-finite values.
Results may differ from a plain program's by a relative error of at most 0.0003.
Values may be sent and summed in bfloat16 or wider, within the bound.
A program may use at most 64 MiB of HBM per device.

v0:
```python
import math

import jax
import jax.numpy as jnp
from jax import lax
from jax.sharding import PartitionSpec as P

G = 48


eps_norm = 1e-06


def from_behind(value, axis, steps):
    count = lax.axis_size(axis)
    pairs = [(source, (source + steps) % count) for source in range(count)]
    return lax.ppermute(value, axis, pairs)


def wedge_terms(offset, length, tilt_min, tilt_max, tilt_axis):
    half_len = G // 2 + 1
    flat_index = offset + lax.iota(jnp.int32, length)
    depth_index = flat_index % half_len
    column = flat_index // half_len % G
    row_index = flat_index // (half_len * G)
    freq_x = jnp.where(row_index < G // 2, row_index, row_index - G)
    freq_y = jnp.where(column < G // 2, column, column - G)
    tilt_coord = jnp.where(tilt_axis[None, :] == 1, freq_x[:, None], freq_y[:, None])
    radial = jnp.abs(tilt_coord).astype(jnp.float32)
    height = jnp.where(tilt_coord >= 0, -depth_index[:, None], depth_index[:, None]).astype(
        jnp.float32
    )
    lower_slope = jnp.tan(tilt_min.astype(jnp.float32) * (math.pi / 180.0))
    upper_slope = jnp.tan(tilt_max.astype(jnp.float32) * (math.pi / 180.0))
    inside = (radial * lower_slope[None, :] <= height) & (height <= radial * upper_slope[None, :])
    wedge_mask = inside.astype(jnp.bfloat16)
    weight = jnp.where((depth_index == 0) | (depth_index == G // 2), 1.0, 2.0).astype(jnp.float32)
    return (wedge_mask, weight)


def masked_power(spectra_block, wedge_mask, weight):
    masked = spectra_block * wedge_mask[None]
    real_part = masked[0].astype(jnp.float32)
    imag_part = masked[1].astype(jnp.float32)
    power = (weight[:, None] * (real_part * real_part + imag_part * imag_part)).astype(jnp.bfloat16)
    return (masked, power)


def shards(spectra, tilt_min, tilt_max, tilt_axis):
    vox_dev = spectra.shape[1]
    block_len = spectra.shape[2]
    cycle_size = lax.axis_size("pa")
    band_len = cycle_size // 2 + 1
    row_share = block_len // lax.axis_size("af")
    offset = lax.axis_index("af") * vox_dev
    my_block = lax.axis_index("pa")

    def block_wedge(block_id):
        row_start = block_id * block_len
        return wedge_terms(
            offset,
            vox_dev,
            lax.dynamic_slice_in_dim(tilt_min, row_start, block_len),
            lax.dynamic_slice_in_dim(tilt_max, row_start, block_len),
            lax.dynamic_slice_in_dim(tilt_axis, row_start, block_len),
        )

    own_mask, weight = block_wedge(my_block)
    own_masked, own_power = masked_power(spectra, own_mask, weight)
    doubled = weight.astype(jnp.bfloat16)[None, :, None]
    left_stack = jnp.concatenate([own_masked * doubled, own_power[None], own_mask[None]], axis=0)

    def right_stack(carried, block_id):
        other_mask = block_wedge(block_id)[0]
        return jnp.concatenate([carried[0:2], other_mask[None], carried[2:3]], axis=0)

    def block_terms(right_ops):
        partial_value = jnp.einsum(
            "gvp,gvq->pgq", left_stack, right_ops, preferred_element_type=jnp.float32
        )
        return jnp.concatenate(
            [partial_value[:, 0:1] + partial_value[:, 1:2], partial_value[:, 2:4]], axis=1
        )

    initial = jnp.concatenate([own_masked, own_power[None]], axis=0)
    first_terms = block_terms(right_stack(initial, my_block))

    def advance(carried, step_index):
        arrived = from_behind(carried, "pa", -1)
        block_id = (my_block + step_index) % cycle_size
        return (arrived, block_terms(right_stack(arrived, block_id)))

    final_carry, later_terms = lax.scan(advance, initial, jnp.arange(1, band_len, dtype=jnp.int32))
    gathered = jnp.concatenate([first_terms[None], later_terms], axis=0)
    gathered = lax.psum_scatter(gathered, "af", scatter_dimension=1, tiled=True)
    cross_sum = gathered[:, :, 0]
    own_norm = gathered[:, :, 1]
    other_norm = gathered[:, :, 2]
    correlation = cross_sum / jnp.sqrt(own_norm * other_norm + eps_norm)
    return jnp.transpose(correlation, (1, 0, 2)).reshape(row_share, band_len * block_len)


def solution(mesh):
    in_specs = (P(None, "af", "pa"), P(), P(), P())
    out_specs = P(("pa", "af"), None)
    return jax.shard_map(shards, mesh=mesh, in_specs=in_specs, out_specs=out_specs, check_vma=False)
```

profile of v0, /device:TPU:4, one launch (start us, length us, event | category | flops | bytes accessed | tf_op | source)
XLA Modules:
  0.0 533.3 jit_solution(6366399166112521183)
XLA Ops:
  8.4 2.8 fusion.44
  11.2 2.8 fusion.42
  14.1 1.9 broadcast_multiply_fusion
  19.2 2.0 pad_maximum_fusion
  23.2 325.7 %while.15 = (s32[]{:T(128)}, bf16[3,3600,128]{2,1,0:T(8,128)(2,1)}, f32[8,128,3,128]{1,3,2,0:T(8,128)}, s32[8]{0:T(128)S(1)}, s32[]{:T(128)}, /*index=5*/s32[204...) while((s32[]{:T(128)}, bf16[3,3600,128]{2,1,0:T(8,128)(2,1)}, ...), condition=%wide.region_1.2_spmd, body=%wide.region_0.1_spmd.sunk | while | flops 481267392 | bytes 46391968 | solution.py:93
  23.2 3.2 collective-permute-start
  29.3 2.8 fusion.69
  32.2 25.2 %collective-permute-done = bf16[3,3600,128]{2,1,0:T(8,128)(2,1)S(1)} collective-permute-done((bf16[3,3600,128]{2,1,0:T(8,128)(2,1)}, bf16[3,3600,128]{2,1,0:T(8,128)(2,1)S(1)}, u32[]{:S(2)}, u32[]{:S(2)}) %collective-permute-start) | collective-permute-done | bytes 2764832 | tf_op jit(solution)/shard_map/while/body/eval_jaxpr/ppermute | solution.py:17
  63.3 3.9 collective-permute-start
  70.1 2.8 fusion.69
  73.0 25.2 %collective-permute-done = bf16[3,3600,128]{2,1,0:T(8,128)(2,1)S(1)} collective-permute-done((bf16[3,3600,128]{2,1,0:T(8,128)(2,1)}, bf16[3,3600,128]{2,1,0:T(8,128)(2,1)S(1)}, u32[]{:S(2)}, u32[]{:S(2)}) %collective-permute-start) | collective-permute-done | bytes 2764832 | tf_op jit(solution)/shard_map/while/body/eval_jaxpr/ppermute | solution.py:17
  104.1 3.9 collective-permute-start
  110.9 2.8 fusion.69
  113.8 25.2 %collective-permute-done = bf16[3,3600,128]{2,1,0:T(8,128)(2,1)S(1)} collective-permute-done((bf16[3,3600,128]{2,1,0:T(8,128)(2,1)}, bf16[3,3600,128]{2,1,0:T(8,128)(2,1)S(1)}, u32[]{:S(2)}, u32[]{:S(2)}) %collective-permute-start) | collective-permute-done | bytes 2764832 | tf_op jit(solution)/shard_map/while/body/eval_jaxpr/ppermute | solution.py:17
  144.9 3.9 collective-permute-start
  151.7 2.8 fusion.69
  154.6 25.2 %collective-permute-done = bf16[3,3600,128]{2,1,0:T(8,128)(2,1)S(1)} collective-permute-done((bf16[3,3600,128]{2,1,0:T(8,128)(2,1)}, bf16[3,3600,128]{2,1,0:T(8,128)(2,1)S(1)}, u32[]{:S(2)}, u32[]{:S(2)}) %collective-permute-start) | collective-permute-done | bytes 2764832 | tf_op jit(solution)/shard_map/while/body/eval_jaxpr/ppermute | solution.py:17
  185.7 3.9 collective-permute-start
  192.5 2.8 fusion.69
  195.4 25.2 %collective-permute-done = bf16[3,3600,128]{2,1,0:T(8,128)(2,1)S(1)} collective-permute-done((bf16[3,3600,128]{2,1,0:T(8,128)(2,1)}, bf16[3,3600,128]{2,1,0:T(8,128)(2,1)S(1)}, u32[]{:S(2)}, u32[]{:S(2)}) %collective-permute-start) | collective-permute-done | bytes 2764832 | tf_op jit(solution)/shard_map/while/body/eval_jaxpr/ppermute | solution.py:17
  226.5 3.9 collective-permute-start
  233.3 2.8 fusion.69
  236.2 25.2 %collective-permute-done = bf16[3,3600,128]{2,1,0:T(8,128)(2,1)S(1)} collective-permute-done((bf16[3,3600,128]{2,1,0:T(8,128)(2,1)}, bf16[3,3600,128]{2,1,0:T(8,128)(2,1)S(1)}, u32[]{:S(2)}, u32[]{:S(2)}) %collective-permute-start) | collective-permute-done | bytes 2764832 | tf_op jit(solution)/shard_map/while/body/eval_jaxpr/ppermute | solution.py:17
  267.3 3.9 collective-permute-start
  274.1 2.8 fusion.69
  277.0 25.2 %collective-permute-done = bf16[3,3600,128]{2,1,0:T(8,128)(2,1)S(1)} collective-permute-done((bf16[3,3600,128]{2,1,0:T(8,128)(2,1)}, bf16[3,3600,128]{2,1,0:T(8,128)(2,1)S(1)}, u32[]{:S(2)}, u32[]{:S(2)}) %collective-permute-start) | collective-permute-done | bytes 2764832 | tf_op jit(solution)/shard_map/while/body/eval_jaxpr/ppermute | solution.py:17
  308.1 3.9 collective-permute-start
  314.9 2.8 fusion.69
  317.8 25.2 %collective-permute-done = bf16[3,3600,128]{2,1,0:T(8,128)(2,1)S(1)} collective-permute-done((bf16[3,3600,128]{2,1,0:T(8,128)(2,1)}, bf16[3,3600,128]{2,1,0:T(8,128)(2,1)S(1)}, u32[]{:S(2)}, u32[]{:S(2)}) %collective-permute-start) | collective-permute-done | bytes 2764832 | tf_op jit(solution)/shard_map/while/body/eval_jaxpr/ppermute | solution.py:17
  348.9 2.4 copy.9
  351.2 2.0 pad_maximum_fusion.2
  355.2 169.5 %all-reduce.3.cloned.1.call-done = f32[9,128,3,128]{3,2,0,1:T(4,128)} async-done(((f32[9,128,3,128]{3,2,0,1:T(4,128)}), f32[9,128,3,128]{3,2,0,1:T(4,128)}) %all-reduce.3.cloned.1.call-update) | async-done | bytes 1769488
  (135 shorter events, 74.6 us)
Async XLA Ops:
  6.5 518.1 %all-reduce.3.cloned.1.call-start = ((), (), s32[]{:S(2)}) async-start(), calls=%async_computation | async-start | bytes 4718592
  6.6 7.5 %copy-start.1 = (bf16[2,3600,128]{2,1,0:T(8,128)(2,1)S(1)}, bf16[2,3600,128]{2,1,0:T(8,128)(2,1)}, u32[]{:S(2)}) copy-start(bf16[2,3600,128]{2,1,0:T(8,128)(2,1)} %param.6) | copy-start | bytes 5529604
  23.2 34.2 %collective-permute-start = (bf16[3,3600,128]{2,1,0:T(8,128)(2,1)}, bf16[3,3600,128]{2,1,0:T(8,128)(2,1)S(1)}, u32[]{:S(2)}, u32[]{:S(2)}) collective-permute-start(bf16[3,3600,128]{2,1,0:T(8,128)(2,1)} %get-tuple-element.314), channel_id=1, source_target_pairs={{0,240},{16,0},{32,16},{48,32},{64,48},{80,64},{96,80},{112,96},{1... | collective-permute-start | bytes 8294408 | tf_op jit(solution)/shard_map/while/body/eval_jaxpr/ppermute | solution.py:17
  57.4 2.0 copy-start
  63.3 34.9 %collective-permute-start = (bf16[3,3600,128]{2,1,0:T(8,128)(2,1)}, bf16[3,3600,128]{2,1,0:T(8,128)(2,1)S(1)}, u32[]{:S(2)}, u32[]{:S(2)}) collective-permute-start(bf16[3,3600,128]{2,1,0:T(8,128)(2,1)} %get-tuple-element.314), channel_id=1, source_target_pairs={{0,240},{16,0},{32,16},{48,32},{64,48},{80,64},{96,80},{112,96},{1... | collective-permute-start | bytes 8294408 | tf_op jit(solution)/shard_map/while/body/eval_jaxpr/ppermute | solution.py:17
  98.2 2.0 copy-start
  104.1 34.9 %collective-permute-start = (bf16[3,3600,128]{2,1,0:T(8,128)(2,1)}, bf16[3,3600,128]{2,1,0:T(8,128)(2,1)S(1)}, u32[]{:S(2)}, u32[]{:S(2)}) collective-permute-start(bf16[3,3600,128]{2,1,0:T(8,128)(2,1)} %get-tuple-element.314), channel_id=1, source_target_pairs={{0,240},{16,0},{32,16},{48,32},{64,48},{80,64},{96,80},{112,96},{1... | collective-permute-start | bytes 8294408 | tf_op jit(solution)/shard_map/while/body/eval_jaxpr/ppermute | solution.py:17
  139.0 2.0 copy-start
  144.9 34.9 %collective-permute-start = (bf16[3,3600,128]{2,1,0:T(8,128)(2,1)}, bf16[3,3600,128]{2,1,0:T(8,128)(2,1)S(1)}, u32[]{:S(2)}, u32[]{:S(2)}) collective-permute-start(bf16[3,3600,128]{2,1,0:T(8,128)(2,1)} %get-tuple-element.314), channel_id=1, source_target_pairs={{0,240},{16,0},{32,16},{48,32},{64,48},{80,64},{96,80},{112,96},{1... | collective-permute-start | bytes 8294408 | tf_op jit(solution)/shard_map/while/body/eval_jaxpr/ppermute | solution.py:17
  179.8 2.0 copy-start
  185.7 34.9 %collective-permute-start = (bf16[3,3600,128]{2,1,0:T(8,128)(2,1)}, bf16[3,3600,128]{2,1,0:T(8,128)(2,1)S(1)}, u32[]{:S(2)}, u32[]{:S(2)}) collective-permute-start(bf16[3,3600,128]{2,1,0:T(8,128)(2,1)} %get-tuple-element.314), channel_id=1, source_target_pairs={{0,240},{16,0},{32,16},{48,32},{64,48},{80,64},{96,80},{112,96},{1... | collective-permute-start | bytes 8294408 | tf_op jit(solution)/shard_map/while/body/eval_jaxpr/ppermute | solution.py:17
  220.6 2.0 copy-start
  226.5 34.9 %collective-permute-start = (bf16[3,3600,128]{2,1,0:T(8,128)(2,1)}, bf16[3,3600,128]{2,1,0:T(8,128)(2,1)S(1)}, u32[]{:S(2)}, u32[]{:S(2)}) collective-permute-start(bf16[3,3600,128]{2,1,0:T(8,128)(2,1)} %get-tuple-element.314), channel_id=1, source_target_pairs={{0,240},{16,0},{32,16},{48,32},{64,48},{80,64},{96,80},{112,96},{1... | collective-permute-start | bytes 8294408 | tf_op jit(solution)/shard_map/while/body/eval_jaxpr/ppermute | solution.py:17
  261.4 2.0 copy-start
  267.3 34.9 %collective-permute-start = (bf16[3,3600,128]{2,1,0:T(8,128)(2,1)}, bf16[3,3600,128]{2,1,0:T(8,128)(2,1)S(1)}, u32[]{:S(2)}, u32[]{:S(2)}) collective-permute-start(bf16[3,3600,128]{2,1,0:T(8,128)(2,1)} %get-tuple-element.314), channel_id=1, source_target_pairs={{0,240},{16,0},{32,16},{48,32},{64,48},{80,64},{96,80},{112,96},{1... | collective-permute-start | bytes 8294408 | tf_op jit(solution)/shard_map/while/body/eval_jaxpr/ppermute | solution.py:17
  302.2 2.0 copy-start
  308.1 34.9 %collective-permute-start = (bf16[3,3600,128]{2,1,0:T(8,128)(2,1)}, bf16[3,3600,128]{2,1,0:T(8,128)(2,1)S(1)}, u32[]{:S(2)}, u32[]{:S(2)}) collective-permute-start(bf16[3,3600,128]{2,1,0:T(8,128)(2,1)} %get-tuple-element.314), channel_id=1, source_target_pairs={{0,240},{16,0},{32,16},{48,32},{64,48},{80,64},{96,80},{112,96},{1... | collective-permute-start | bytes 8294408 | tf_op jit(solution)/shard_map/while/body/eval_jaxpr/ppermute | solution.py:17
  343.0 2.0 copy-start
  353.2 0.7 copy-start.2
Sparse Core Ops, SparseCore 0:
  353.4 171.2 all-reduce.2
where the time goes:
time: 536 us; the launch traced here: 533 us
  waiting for transfers between devices  371 us (69%)
  other arithmetic  59.2 us (11%)
  local copies, waits for them, and re-layouts  38.2 us (7%)
  starting transfers between devices  30.5 us (6%)
  between operations  14.2 us (3%)
  matrix products  13.9 us (3%)
  loops' own time  5.84 us (1%)
    ppermute x8, waiting for transfers between devices, from_behind(): return lax.ppermute(value, axis, pairs)  202 us
    unnamed x2, waiting for transfers between devices  170 us
    ppermute x8, starting transfers between devices, from_behind(): return lax.ppermute(value, axis, pairs)  30.5 us
    convert_element_type x10, other arithmetic, wedge_terms(): wedge_mask = inside.astype(jnp.bfloat16)  28.5 us
    while x24, local copies, waits for them, and re-layouts  27.1 us
    dot_general x9, matrix products, block_terms(): jnp.einsum('gvp,gvq->pgq', left_stack, right_ops, preferred_element_type=...  13.9 us
  transfers between devices with their start and end apart: 9, of which 9 were waited for; matrix products, arithmetic and copies ran while one was open for 8% of the time, Pallas kernels for 0%

commit v1 on v0

v1 whole, which is shorter than its diff:
```python
import functools
import math

import jax
import jax.numpy as jnp
from jax import lax
from jax.experimental import pallas as pl
from jax.experimental.pallas import tpu as pltpu
from jax.sharding import PartitionSpec as P

MESH = pl.DeviceIdType.MESH
F32 = jnp.float32
BF16 = jnp.bfloat16

G = 48
HALF = 25
VD = 3600
KC = 1824
A = 928
B = 896
FA = A // 2
FB = B // 2
CH = 96
T_LO, T_HI, N_T = 46, 70, 25
eps_norm = 1e-06


def coords():
    pa = lax.axis_index("pa")
    af = lax.axis_index("af")
    return pa // 8, (pa // 2) % 4, pa % 2, af // 2, af % 2


def dev(xl, y, core, z, xh):
    return {"pa": (xl * 4 + y) * 2 + core, "af": z * 2 + xh}


def tdot(lhs, rhs):
    return lax.dot_general(lhs, rhs, (((0,), (0,)), ((), ())), preferred_element_type=F32)


def cells(first, shape):
    v = (first + lax.broadcasted_iota(jnp.int32, shape, 0)).astype(F32)
    q = jnp.floor((v + 0.5) * (1.0 / HALF))
    iz = v - q * HALF
    ix = jnp.floor((q + 0.5) * (1.0 / G))
    iy = q - ix * G
    fx = jnp.where(ix < G // 2, ix, ix - G)
    fy = jnp.where(iy < G // 2, iy, iy - G)
    return fx, fy, iz


def kernel(spec_hbm, cols_ref, out_ref, m, o, ow, ra, rb, fa, fb, acc, inc, zl, rz, fin, load_sem, ssem, rsem):
    xl, y, core, z, xh = coords()
    af = lax.axis_index("af")
    yp, ym, y2 = (y + 1) % 4, (y + 3) % 4, (y + 2) % 4
    zp, zm = (z + 1) % 8, (z + 7) % 8
    started = []

    def rdma(src, dst, target):
        i = len(started)
        c = pltpu.make_async_remote_copy(
            src_ref=src, dst_ref=dst, send_sem=ssem.at[i], recv_sem=rsem.at[i], device_id=target, device_id_type=MESH
        )
        c.start()
        started.append(c)
        return c

    loads = [
        pltpu.make_async_copy(spec_hbm.at[p], m.at[p, pl.ds(0, VD)], load_sem.at[p]) for p in range(2)
    ]
    for c in loads:
        c.start()
    barrier = pltpu.get_barrier_semaphore()
    peers = [
        dev(xl, y, 1 - core, z, xh),
        dev(1 - xl, y, core, z, xh),
        dev(1 - xl, y, 1 - core, z, xh),
        dev(xl, yp, core, z, xh),
        dev(xl, ym, core, z, xh),
        dev(1 - xl, y, core, z, 1 - xh),
        dev(xl, y, core, zp, xh),
        dev(xl, y, core, zm, xh),
    ]
    for peer in peers:
        pl.semaphore_signal(barrier, inc=1, device_id=peer, device_id_type=MESH)
    m[:, VD:, :] = jnp.zeros((2, 2 * KC - VD, 128), BF16)
    for c in loads:
        c.wait()

    def own_col(dx, dc):
        return pl.multiple_of(((xl ^ dx) * 2 + (core ^ dc)) * 128, 128)

    lower = cols_ref[0:1, :]
    upper = cols_ref[1:2, :]
    axis = cols_ref[2:3, :]

    def mask_half(half):
        def body(i, carry):
            r0 = pl.multiple_of(half * KC + i * CH, 16)
            fx, fy, iz = cells(af * VD + r0, (CH, 128))
            u = jnp.where(axis > 0.5, fx, fy)
            a = jnp.abs(u)
            b = jnp.where(u >= 0.0, -iz, iz)
            keep = ((a * lower <= b) & (b <= a * upper)).astype(F32)
            for p in range(2):
                m[p, pl.ds(r0, CH), :] = (m[p, pl.ds(r0, CH), :].astype(F32) * keep).astype(BF16)
            return carry

        lax.fori_loop(0, KC // CH, body, 0)

    mask_half(core)
    pl.semaphore_wait(barrier, len(peers))

    mine = pl.multiple_of(core * KC, 16)
    theirs = pl.multiple_of((1 - core) * KC, 16)
    col = own_col(0, 0)
    o[:, pl.ds(col, 128)] = m[xl, pl.ds(mine, KC), :]

    y1 = [None] * 4

    def y_send(p):
        c = own_col(p // 2, p % 2)
        y1[p] = (
            rdma(o.at[pl.ds(0, A), pl.ds(c, 128)], ra.at[:, pl.ds(c, 128)], dev(xl, ym, core, z, xh)),
            rdma(o.at[pl.ds(A, B), pl.ds(c, 128)], rb.at[:, pl.ds(c, 128)], dev(xl, yp, core, z, xh)),
        )

    y_send(0)
    x_same = rdma(m.at[1 - xl, pl.ds(mine, KC)], o.at[:, pl.ds(col, 128)], dev(1 - xl, y, core, z, xh))
    mask_half(1 - core)
    sib = rdma(m.at[xl, pl.ds(theirs, KC)], o.at[:, pl.ds(col, 128)], dev(xl, y, 1 - core, z, xh))
    x_other = rdma(m.at[1 - xl, pl.ds(theirs, KC)], o.at[:, pl.ds(col, 128)], dev(1 - xl, y, 1 - core, z, xh))

    y_2 = [None] * 4

    def forward(p):
        c = own_col(p // 2, p % 2)
        for d in y1[p]:
            d.wait_recv()
        to_m = pl.multiple_of(jnp.where(ym < 2, 0, FA), 16)
        to_p = pl.multiple_of(jnp.where(yp < 2, 0, FB), 16)
        y_2[p] = (
            rdma(ra.at[pl.ds(to_m, FA), pl.ds(c, 128)], fa.at[:, pl.ds(c, 128)], dev(xl, ym, core, z, xh)),
            rdma(rb.at[pl.ds(to_p, FB), pl.ds(c, 128)], fb.at[:, pl.ds(c, 128)], dev(xl, yp, core, z, xh)),
        )

    sib.wait_recv()
    y_send(1)
    forward(0)
    x_same.wait_recv()
    y_send(2)
    forward(1)
    x_other.wait_recv()
    y_send(3)

    def weigh(i, carry):
        r0 = pl.multiple_of(i * CH, 16)
        iz = cells(af * VD + core * KC + r0, (CH, 128))[2]
        w = jnp.where((iz < 0.5) | (iz > 23.5), 1.0, 2.0)
        for q in range(4):
            ow[pl.ds(r0, CH), q * 128 : (q + 1) * 128] = (
                o[pl.ds(r0, CH), q * 128 : (q + 1) * 128].astype(F32) * w
            ).astype(BF16)
        return carry

    lax.fori_loop(0, KC // CH, weigh, 0)

    def put(tile, value):
        acc[tile] = value.reshape(2, 128, 256)

    def side(x):
        return pl.multiple_of(x * 256, 256)

    def wrap(x, cond):
        return x ^ cond.astype(jnp.int32)

    for x in range(2):
        for slot, xo in ((0, x), (4, 1 - x)):
            put(x * 8 + slot, tdot(ow[:, x * 256 : x * 256 + 256], o[:, xo * 256 : xo * 256 + 256]))

    forward(2)
    forward(3)
    for x in range(2):
        put(x * 8 + 1, tdot(ow[0:A, x * 256 : x * 256 + 256], ra[:, pl.ds(side(wrap(x, y == 3)), 256)]))
        put(x * 8 + 5, tdot(ra[:, x * 256 : x * 256 + 256], ow[0:A, pl.ds(side(wrap(1 - x, y == 3)), 256)]))
        put(x * 8 + 3, tdot(ow[A:KC, x * 256 : x * 256 + 256], rb[:, pl.ds(side(wrap(1 - x, y == 0)), 256)]))
        put(x * 8 + 6, tdot(rb[:, x * 256 : x * 256 + 256], ow[A:KC, pl.ds(side(wrap(x, y == 0)), 256)]))

    for p in range(4):
        for d in y_2[p]:
            d.wait_recv()
    at_a = pl.multiple_of(jnp.where(y < 2, 0, FA), 16)
    at_b = pl.multiple_of(A + jnp.where(y < 2, 0, FB), 16)
    for x in range(2):
        mine_x = side(wrap(x, y >= 2))
        other_x = side(wrap(x, y < 2))
        put(
            x * 8 + 2,
            tdot(ow[pl.ds(at_a, FA), x * 256 : x * 256 + 256], fa[:, pl.ds(mine_x, 256)])
            + tdot(ow[pl.ds(at_b, FB), x * 256 : x * 256 + 256], fb[:, pl.ds(mine_x, 256)]),
        )
        put(
            x * 8 + 7,
            tdot(fa[:, x * 256 : x * 256 + 256], ow[pl.ds(at_a, FA), pl.ds(other_x, 256)])
            + tdot(fb[:, x * 256 : x * 256 + 256], ow[pl.ds(at_b, FB), pl.ds(other_x, 256)]),
        )

    pair = rdma(acc.at[:, 1 - core], inc, dev(xl, y, 1 - core, z, xh))
    pair.wait_recv()
    for t in range(16):
        inc[t] = inc[t] + acc[t, core]

    def rows(zz):
        return pl.ds(pl.multiple_of(((zz + 16) % 8) * 16, 16), 16)

    flows = []
    for lo, way, steps in ((0, 1, 3), (0, -1, 4), (8, 1, 4), (8, -1, 3)):
        flows.append(dict(lo=lo, way=way, steps=steps, target=dev(xl, y, core, zp if way > 0 else zm, xh)))
    for s in range(4):
        for f, flow in enumerate(flows):
            if s >= flow["steps"]:
                continue
            tiles = pl.ds(flow["lo"], 8)
            here = rows(z + flow["way"] * (flow["steps"] - s))
            if s == 0:
                src = inc.at[tiles, here]
            else:
                flow["copy"].wait_recv()
                src = zl.at[f, s - 1]
                src[...] = src[...] + inc[tiles, here, :]
            flow["copy"] = rdma(src, zl.at[f, s], flow["target"])
    for flow in flows:
        flow["copy"].wait_recv()
    for f in (0, 2):
        lo = flows[f]["lo"]
        rz[lo : lo + 8] = (
            inc[lo : lo + 8, rows(z), :]
            + zl[f, flows[f]["steps"] - 1]
            + zl[f + 1, flows[f + 1]["steps"] - 1]
        )

    me_x = xh * 2 + xl
    last = []
    for dx in range(4):
        xo = xl ^ (dx % 2)
        ho = xh ^ (dx // 2)
        here = pl.ds(pl.multiple_of(ho * 8, 8), 8)
        base = xo * 8
        if dx:
            last.append(rdma(rz.at[pl.ds(base, 5), here], fin.at[me_x, 0:5], dev(xo, y, core, z, ho)))
        else:
            fin[me_x, 0:5] = rz[pl.ds(base, 5), here, :]
        for slot, yo in ((5, yp), (6, ym), (7, y2)):
            last.append(rdma(rz.at[base + slot, here], fin.at[me_x, slot], dev(xo, yo, core, z, ho)))
    for c in last:
        c.wait_recv()
    s = [fin[0, t] + fin[1, t] + fin[2, t] + fin[3, t] for t in range(8)]
    parts = [s[0], s[1] + s[6], s[2] + s[7], s[3] + s[5], s[4]]
    for g in range(5):
        out_ref[:, g * 256 : (g + 1) * 256] = parts[g]
    for c in started:
        c.wait_send()


def cross_call(spectra, cols):
    scratch = [
        pltpu.VMEM((2, 2 * KC, 128), BF16),
        pltpu.VMEM((KC, 512), BF16),
        pltpu.VMEM((KC, 512), BF16),
        pltpu.VMEM((A, 512), BF16),
        pltpu.VMEM((B, 512), BF16),
        pltpu.VMEM((FA, 512), BF16),
        pltpu.VMEM((FB, 512), BF16),
        pltpu.VMEM((16, 2, 128, 256), F32),
        pltpu.VMEM((16, 128, 256), F32),
        pltpu.VMEM((4, 4, 8, 16, 256), F32),
        pltpu.VMEM((16, 16, 256), F32),
        pltpu.VMEM((4, 8, 8, 256), F32),
        pltpu.SemaphoreType.DMA((2,)),
        pltpu.SemaphoreType.DMA((64,)),
        pltpu.SemaphoreType.DMA((64,)),
    ]
    return pl.pallas_call(
        kernel,
        out_shape=jax.ShapeDtypeStruct((8, 1280), F32),
        in_specs=[pl.BlockSpec(memory_space=pl.ANY), pl.BlockSpec(memory_space=pltpu.VMEM)],
        out_specs=pl.BlockSpec(memory_space=pltpu.VMEM),
        scratch_shapes=scratch,
        compiler_params=pltpu.CompilerParams(
            collective_id=0, has_side_effects=True, vmem_limit_bytes=56 * 2**20
        ),
    )(spectra, cols)


def slopes(degrees):
    return jnp.tan(degrees.astype(F32) * (math.pi / 180.0))


def shards(spectra, tilt_min, tilt_max, tilt_axis):
    pa = lax.axis_index("pa")
    af = lax.axis_index("af")
    lower, upper = slopes(tilt_min), slopes(tilt_max)

    def own(value):
        return lax.dynamic_slice_in_dim(value, pa * 128, 128)

    cols = jnp.zeros((8, 128), F32)
    cols = cols.at[0].set(own(lower)).at[1].set(own(upper)).at[2].set(own(tilt_axis).astype(F32))
    cross = cross_call(spectra, cols)

    fx, fy, iz = cells(af * VD, (VD, 128))
    u = jnp.where(cols[2] > 0.5, fx, fy)
    a = jnp.abs(u)
    b = jnp.where(u >= 0, -iz, iz)
    keep = (a * cols[0] <= b) & (b <= a * cols[1])
    w = jnp.where((iz < 0.5) | (iz > 23.5), 1.0, 2.0)
    real, imag = spectra[0].astype(F32), spectra[1].astype(F32)
    power = jnp.where(keep, w * (real * real + imag * imag), 0.0).astype(BF16)
    lane = jnp.arange(128)
    c_axis, c_side, c_t = lane // 50, (lane // 25) % 2, (lane % 25)
    slope = slopes(c_t + T_LO)
    cu = jnp.where(c_axis == 1, fx, fy)
    c_keep = (
        (iz <= jnp.abs(cu) * slope) & ((cu >= 0) == (c_side == 0)) & (lane < 100)
    ).astype(BF16)
    table = jnp.einsum("vi,vc->ic", power, c_keep, preferred_element_type=F32)
    table = lax.psum(table, "af")
    table = lax.all_gather(table, "pa", tiled=True)

    def hot(t_min, t_max, axis):
        first = axis * 50 + (-t_min - T_LO)
        second = axis * 50 + 25 + (t_max - T_LO)
        return ((lane == first[:, None]) | (lane == second[:, None])).astype(F32)

    hots = hot(tilt_min, tilt_max, tilt_axis)
    band = (pa * 128 + jnp.arange(1152)) % 2048
    row0 = pa * 128 + af * 8
    t_own = lax.dynamic_slice_in_dim(table, row0, 8)
    h_own = lax.dynamic_slice_in_dim(hots, row0, 8)
    highest = lax.Precision.HIGHEST
    own_norm = jnp.einsum("ic,jc->ij", t_own, hots[band], precision=highest)
    other_norm = jnp.einsum("ic,jc->ij", h_own, table[band], precision=highest)
    cross = lax.dynamic_slice_in_dim(cross, (pa % 2) * 128, 1152, 1)
    return cross / jnp.sqrt(own_norm * other_norm + eps_norm)


def solution(mesh):
    in_specs = (P(None, "af", "pa"), P(), P(), P())
    out_specs = P(("pa", "af"), None)
    return jax.shard_map(shards, mesh=mesh, in_specs=in_specs, out_specs=out_specs, check_vma=False)
```

time: 536 us -> 271 us (0.51)
  waiting for transfers between devices: 371 us -> 152 us
  Pallas kernels: 0 us -> 76.6 us
  other arithmetic: 59.2 us -> 3.77 us
  local copies, waits for them, and re-layouts: 38.2 us -> 6.47 us
  starting transfers between devices: 30.5 us -> 0.04 us
  loops' own time: 5.84 us -> 0 us
    ppermute x8 -> x0, waiting for transfers between devices: 202 us -> none  [from_behind(): return lax.ppermute(value, axis, pairs)]
    unnamed x2, waiting for transfers between devices: 170 us -> 0.03 us
    psum x0 -> x1, waiting for transfers between devices: none -> 152 us  [shards(): table = lax.psum(table, 'af')]
    pallas_call x0 -> x1, Pallas kernels: none -> 76.6 us  [cross_call(): pl.pallas_call(kernel, out_shape=jax.ShapeDtypeStruct((8, 1280), F32), in...]
    ppermute x8 -> x0, starting transfers between devices: 30.5 us -> none  [from_behind(): return lax.ppermute(value, axis, pairs)]
    convert_element_type x11 -> x0, other arithmetic: 30.1 us -> none  [the longest x10 28.5 us: wedge_terms(): wedge_mask = inside.astype(jnp.bfloat16)]
    while x25 -> x0, local copies, waits for them, and re-layouts: 29.5 us -> none
    tan x9 -> x1, other arithmetic: 7.44 us -> 0.05 us  [slopes(): return jnp.tan(degrees.astype(F32) * (math.pi / 180.0))]
  transfers between devices with their start and end apart: 9 -> 2, of which waited for: 9 -> 1; matrix products, arithmetic and copies ran while one was open for 8% -> 1% of each run, Pallas kernels for 0% -> 29%
where the time goes in v1:
time: 271 us; the launch traced here: 268 us
  waiting for transfers between devices  152 us (56%)
  Pallas kernels  76.6 us (28%)
  matrix products  15.7 us (6%)
  between operations  13.6 us (5%)
  local copies, waits for them, and re-layouts  6.47 us (2%)
  other arithmetic  3.77 us (1%)
    psum x1, waiting for transfers between devices, shards(): table = lax.psum(table, 'af')  152 us
    pallas_call x1, Pallas kernels, cross_call(): pl.pallas_call(kernel, out_shape=jax.ShapeDtypeStruct((8, 1280), F32), in...  76.6 us
    dot_general x1, matrix products, shards(): table = jnp.einsum('vi,vc->ic', power, c_keep, preferred_element_type=F32)  13.6 us
  transfers between devices with their start and end apart: 2, of which 1 were waited for; matrix products, arithmetic and copies ran while one was open for 1% of the time, Pallas kernels for 29%

profile of v1, /device:TPU:4, one launch (start us, length us, event | category | flops | bytes accessed | tf_op | source)
XLA Modules:
  0.0 268.4 jit_solution(2300499814041131019)
XLA Ops:
  6.5 0.0 all-reduce.3.cloned.1.call-start
  6.5 0.1 fusion.48
  6.7 0.8 convert_bitcast_fusion
  7.5 0.8 iota_compare_fusion.2
  8.2 0.8 fusion.55
  9.2 0.0 copy-start.1
  9.2 13.6 %fusion.17 = f32[128,128]{1,0:T(8,128)} fusion(f32[128]{0:T(128)S(1)} %fusion.48, f32[3600]{0:T(1024)S(1)} %get-tuple-element.47, bf16[2,3600,128]{2,1,0:T(8,128)(2,1)} %spec_hbm.1, f32[3600]{0:T(1024)S(1)} %get-tuple-element.50, f32[128]{0:T(128)S(1)} %get-tuple-element.44, f32[3600]{0:T(1024)S(1)} %fusion.36, f32[128]{0:T(128)S(1)} %get-tuple-element.43, ...), kind=kOutput, calls=%fused_computation.25 | convolution fusion | flops 131328000 | bytes 2125312 | tf_op jit(solution)/shard_map/vi,vc->ic/dot_general | solution.py:327
  22.8 0.0 copy-done.1
  22.8 0.0 copy-start.2
  22.8 0.0 copy-start.3
  22.8 0.0 copy-start.4
  22.9 0.0 all-reduce.3.cloned.1.call-update
  22.9 0.0 all-gather.2.cloned.1.call-start
  22.9 152.1 %all-reduce.3.cloned.1.call-done = f32[128,128]{1,0:T(8,128)} async-done(((f32[128,128]{1,0:T(8,128)}), f32[128,128]{1,0:T(8,128)}) %all-reduce.3.cloned.1.call-update) | async-done | bytes 65552 | tf_op jit(solution)/shard_map/psum | solution.py:328
  175.0 0.0 all-gather.2.cloned.1.call-update
  175.1 76.6 %shard_map.46 = f32[8,1280]{1,0:T(8,128)} custom-call(bf16[2,3600,128]{2,1,0:T(8,128)(2,1)} %spec_hbm.1, f32[8,128]{1,0:T(8,128)} %copy-done.1), custom_call_target="tpu_custom_call" | custom-call | tf_op jit(solution)/shard_map/pallas_call | solution.py:284
  251.8 0.0 copy-done.2
  251.8 0.0 copy-done.3
  251.8 0.0 copy-done.4
  251.8 1.2 fusion.19
  253.0 2.7 %gather_fusion = pred[1152,128]{1,0:T(32,128)(4,1)S(1)} fusion(pred[2048,128]{1,0:T(8,128)(4,1)S(1)} %fusion.19, s32[2048]{0:T(1024)S(1)} %pad_clamp_fusion), kind=kCustom, calls=%fused_computation | custom fusion | bytes 299520 | tf_op jit(solution)/shard_map/gather | solution.py:342
  255.7 0.0 copy-start
  255.7 0.0 all-gather.2.cloned.1.call-done
  255.8 3.7 %gather_fusion.1 = f32[1152,128]{1,0:T(8,128)S(1)} fusion(f32[2048,128]{1,0:T(8,128)} %all-gather.2.cloned.1.call-done, s32[2048]{0:T(1024)S(1)} %pad_clamp_fusion), kind=kCustom, calls=%fused_computation.1 | custom fusion | bytes 1184256 | tf_op jit(solution)/shard_map/gather | solution.py:343
  259.4 1.0 fusion.39
  260.5 0.0 copy-done
  260.5 1.1 fusion.8
  (13 shorter events, 0.2 us)
Async XLA Ops:
  6.5 168.5 %all-reduce.3.cloned.1.call-start = ((), (), s32[]{:S(2)}) async-start(), calls=%async_computation | async-start | bytes 131072 | tf_op jit(solution)/shard_map/psum | solution.py:328
  9.2 13.7 %copy-start.1 = (f32[8,128]{1,0:T(8,128)}, f32[8,128]{1,0:T(8,128)S(1)}, u32[]{:S(2)}) copy-start(f32[8,128]{1,0:T(8,128)S(1)} %scatter.14.cols_ref) | copy-start | bytes 12292
  22.8 228.9 %copy-start.2 = (s32[2048]{0:T(1024)S(1)}, s32[2048]{0:T(1024)}, u32[]{:S(2)}) copy-start(s32[2048]{0:T(1024)} %param.11) | copy-start | bytes 24580
  22.8 228.9 %copy-start.3 = (s32[2048]{0:T(1024)S(1)}, s32[2048]{0:T(1024)}, u32[]{:S(2)}) copy-start(s32[2048]{0:T(1024)} %param.13) | copy-start | bytes 24580
  22.8 228.9 %copy-start.4 = (s32[2048]{0:T(1024)S(1)}, s32[2048]{0:T(1024)}, u32[]{:S(2)}) copy-start(s32[2048]{0:T(1024)} %param.12) | copy-start | bytes 24580
  22.9 232.9 %all-gather.2.cloned.1.call-start = ((), (), s32[]{:S(2)}) async-start(), calls=%async_computation.1 | async-start | bytes 1114112 | tf_op jit(solution)/shard_map/all_gather | solution.py:329
  255.7 4.7 %copy-start = (f32[8,1280]{1,0:T(8,128)S(1)}, f32[8,1280]{1,0:T(8,128)}, u32[]{:S(2)}) copy-start(f32[8,1280]{1,0:T(8,128)} %shard_map.46) | copy-start | bytes 122884
Sparse Core Ops, SparseCore 0:
  23.0 151.9 all-reduce.2
  177.0 34.7 all-gather.1

commit v2 on v1

v2 whole, which is shorter than its diff:
```python
import functools
import math

import jax
import jax.numpy as jnp
from jax import lax
from jax.experimental import pallas as pl
from jax.experimental.pallas import tpu as pltpu
from jax.sharding import PartitionSpec as P

MESH = pl.DeviceIdType.MESH
F32 = jnp.float32
BF16 = jnp.bfloat16

G = 48
HALF = 25
VD = 3600
KC = 1824
A = 928
B = 896
FA = A // 2
FB = B // 2
CH = 96
T_LO, T_HI, N_T = 46, 70, 25
eps_norm = 1e-06


def coords():
    pa = lax.axis_index("pa")
    af = lax.axis_index("af")
    return pa // 8, (pa // 2) % 4, pa % 2, af // 2, af % 2


def dev(xl, y, core, z, xh):
    return {"pa": (xl * 4 + y) * 2 + core, "af": z * 2 + xh}


def tdot(lhs, rhs):
    return lax.dot_general(lhs, rhs, (((0,), (0,)), ((), ())), preferred_element_type=F32)


def cells(first, shape):
    v = (first + lax.broadcasted_iota(jnp.int32, shape, 0)).astype(F32)
    q = jnp.floor((v + 0.5) * (1.0 / HALF))
    iz = v - q * HALF
    ix = jnp.floor((q + 0.5) * (1.0 / G))
    iy = q - ix * G
    fx = jnp.where(ix < G // 2, ix, ix - G)
    fy = jnp.where(iy < G // 2, iy, iy - G)
    return fx, fy, iz

N_SEM = 176


def kernel(spec_hbm, tmin_ref, tmax_ref, axis_ref, out_ref, m, o, ow, ra, rb, fa, fb, acc, inc, xin, zl, rz,
           fin0, fin1, fin2, pw, cm, tt, tl, tg, tf, cls, hot, own, nsend, oth, cross, load_sem, ssem, rsem):
    xl, y, core, z, xh = coords()
    pa = lax.axis_index("pa")
    af = lax.axis_index("af")
    yp, ym, y2 = (y + 1) % 4, (y + 3) % 4, (y + 2) % 4
    zp, zm = (z + 1) % 8, (z + 7) % 8
    me_x = xh * 2 + xl
    started = []

    def rdma(src, dst, target):
        i = len(started)
        c = pltpu.make_async_remote_copy(
            src_ref=src, dst_ref=dst, send_sem=ssem.at[i], recv_sem=rsem.at[i], device_id=target, device_id_type=MESH
        )
        c.start()
        started.append(c)
        return c

    loads = [
        pltpu.make_async_copy(spec_hbm.at[p], m.at[p, pl.ds(0, VD)], load_sem.at[p]) for p in range(2)
    ]
    for c in loads:
        c.start()
    barrier = pltpu.get_barrier_semaphore()
    peers = [
        dev(xl, y, 1 - core, z, xh),
        dev(1 - xl, y, core, z, xh),
        dev(1 - xl, y, 1 - core, z, xh),
        dev(xl, yp, core, z, xh),
        dev(xl, ym, core, z, xh),
        dev(xl, y, core, z, 1 - xh),
        dev(xl, y, core, zp, xh),
        dev(xl, y, core, zm, xh),
    ]
    for peer in peers:
        pl.semaphore_signal(barrier, inc=1, device_id=peer, device_id_type=MESH)
    m[:, VD:, :] = jnp.zeros((2, 2 * KC - VD, 128), BF16)

    cls[0] = axis_ref[...] * 50 + (-T_LO - tmin_ref[...])
    cls[1] = axis_ref[...] * 50 + (N_T - T_LO + tmax_ref[...])
    lower = slopes(tmin_ref[pl.ds(pa, 1), :])
    upper = slopes(tmax_ref[pl.ds(pa, 1), :])
    axis = axis_ref[pl.ds(pa, 1), :]
    lane = lax.broadcasted_iota(jnp.int32, (1, 128), 1)
    c_axis = (lane >= 50).astype(jnp.int32)
    c_side = ((lane - c_axis * 50) >= 25).astype(jnp.int32)
    c_slope = slopes(lane - c_axis * 50 - c_side * 25 + T_LO)
    c_slope = jnp.where(lane < 100, c_slope, -1.0)

    for c in loads:
        c.wait()

    def own_col(dx, dc):
        return pl.multiple_of(((xl ^ dx) * 2 + (core ^ dc)) * 128, 128)

    def mask_half(half):
        def body(i, carry):
            r0 = pl.multiple_of(half * KC + i * CH, 16)
            fx, fy, iz = cells(af * VD + r0, (CH, 128))
            u = jnp.where(axis == 1, fx, fy)
            a = jnp.abs(u)
            b = jnp.where(u >= 0.0, -iz, iz)
            keep = ((a * lower <= b) & (b <= a * upper)).astype(F32)
            for p in range(2):
                m[p, pl.ds(r0, CH), :] = (m[p, pl.ds(r0, CH), :].astype(F32) * keep).astype(BF16)
            return carry

        lax.fori_loop(0, KC // CH, body, 0)

    mask_half(core)
    pl.semaphore_wait(barrier, len(peers))

    mine = pl.multiple_of(core * KC, 16)
    theirs = pl.multiple_of((1 - core) * KC, 16)
    col = own_col(0, 0)
    o[:, pl.ds(col, 128)] = m[xl, pl.ds(mine, KC), :]

    y1a = [[] for _ in range(4)]
    y1b = [[] for _ in range(4)]

    def send_a(p, r0, n):
        c = own_col(p // 2, p % 2)
        y1a[p].append(
            rdma(o.at[pl.ds(r0, n), pl.ds(c, 128)], ra.at[pl.ds(r0, n), pl.ds(c, 128)], dev(xl, ym, core, z, xh))
        )

    def send_b(p, r0, n):
        c = own_col(p // 2, p % 2)
        y1b[p].append(
            rdma(o.at[pl.ds(A + r0, n), pl.ds(c, 128)], rb.at[pl.ds(r0, n), pl.ds(c, 128)], dev(xl, yp, core, z, xh))
        )

    def to_x(r0, n, first, target):
        rows = pl.ds(pl.multiple_of(first + r0, 16), n)
        return rdma(m.at[1 - xl, rows], o.at[pl.ds(r0, n), pl.ds(col, 128)], target)

    send_a(0, 0, A)
    send_b(0, 0, B)
    x_same = [to_x(r0, n, mine, dev(1 - xl, y, core, z, xh)) for r0, n in ((0, A), (A, B))]
    mask_half(1 - core)
    sib = rdma(m.at[xl, pl.ds(theirs, KC)], o.at[:, pl.ds(col, 128)], dev(xl, y, 1 - core, z, xh))
    x_other = [
        to_x(r0, n, theirs, dev(1 - xl, y, 1 - core, z, xh))
        for r0, n in ((0, FA), (A, FB), (FA, FA), (A + FB, FB))
    ]

    def powers(i, carry):
        r0 = pl.multiple_of(i * CH, 16)
        fx, fy, iz = cells(af * VD + r0, (CH, 128))
        re = m[0, pl.ds(r0, CH), :].astype(F32)
        im = m[1, pl.ds(r0, CH), :].astype(F32)
        w = jnp.where((iz < 0.5) | (iz > 23.5), 1.0, 2.0)
        pw[pl.ds(r0, CH), :] = (w * (re * re + im * im)).astype(BF16)
        u = jnp.where(c_axis == 1, fx, fy)
        side = (u < 0.0).astype(jnp.int32)
        cm[pl.ds(r0, CH), :] = ((iz <= jnp.abs(u) * c_slope) & (side == c_side) & (lane < 100)).astype(F32).astype(BF16)
        return carry

    lax.fori_loop(0, 2 * KC // CH, powers, 0)
    tt[...] = tdot(pw[...], cm[...])

    def rows16(zz):
        return pl.ds(pl.multiple_of(((zz + 16) % 8) * 16, 16), 16)

    up, down = dev(xl, y, core, zp, xh), dev(xl, y, core, zm, xh)
    t_flows = [dict(way=1, steps=3, target=up), dict(way=-1, steps=4, target=down)]

    def t_step(s):
        for f, flow in enumerate(t_flows):
            if s > flow["steps"]:
                continue
            if s:
                flow["copy"].wait_recv()
            if s == flow["steps"]:
                continue
            here = rows16(z + flow["way"] * (flow["steps"] - s))
            if s == 0:
                src = tt.at[here]
            else:
                src = tl.at[f, s - 1]
                src[...] = src[...] + tt[here, :]
            flow["copy"] = rdma(src, tl.at[f, s], flow["target"])

    t_step(0)

    y_2 = [None] * 4

    def forward(p):
        c = own_col(p // 2, p % 2)
        to_m = pl.multiple_of(jnp.where(ym < 2, 0, FA), 16)
        to_p = pl.multiple_of(jnp.where(yp < 2, 0, FB), 16)
        for d in y1a[p]:
            d.wait_recv()
        first = rdma(ra.at[pl.ds(to_m, FA), pl.ds(c, 128)], fa.at[:, pl.ds(c, 128)], dev(xl, ym, core, z, xh))
        for d in y1b[p]:
            d.wait_recv()
        second = rdma(rb.at[pl.ds(to_p, FB), pl.ds(c, 128)], fb.at[:, pl.ds(c, 128)], dev(xl, yp, core, z, xh))
        y_2[p] = (first, second)

    sib.wait_recv()
    send_a(1, 0, A)
    send_b(1, 0, B)
    t_step(1)
    forward(0)
    t_step(2)
    x_same[0].wait_recv()
    send_a(2, 0, A)
    x_same[1].wait_recv()
    send_b(2, 0, B)
    t_step(3)
    forward(1)
    t_step(4)
    mine16 = rows16(z)
    tg[xh, mine16, :] = tt[mine16, :] + tl[0, 2] + tl[1, 3]
    gather = []
    for dz in range(8):
        for dh in range(2):
            if dz or dh:
                part = tg.at[xh, mine16]
                gather.append(rdma(part, part, dev(xl, y, core, (z + dz) % 8, xh ^ dh)))

    for d, (send, r0, n) in zip(
        x_other, ((send_a, 0, FA), (send_b, 0, FB), (send_a, FA, FA), (send_b, FB, FB)), strict=True
    ):
        d.wait_recv()
        send(3, r0, n)

    def weigh(i, carry):
        r0 = pl.multiple_of(i * CH, 16)
        iz = cells(af * VD + core * KC + r0, (CH, 128))[2]
        w = jnp.where((iz < 0.5) | (iz > 23.5), 1.0, 2.0)
        for q in range(4):
            ow[pl.ds(r0, CH), q * 128 : (q + 1) * 128] = (
                o[pl.ds(r0, CH), q * 128 : (q + 1) * 128].astype(F32) * w
            ).astype(BF16)
        return carry

    lax.fori_loop(0, KC // CH, weigh, 0)

    def put(tile, value):
        acc[tile] = value.reshape(2, 8, 2, 8, 256)

    def side(x):
        return pl.multiple_of(x * 256, 256)

    def wrap(x, cond):
        return x ^ cond.astype(jnp.int32)

    def pair_sum(lo, n):
        tiles = pl.ds(lo, n)
        return rdma(acc.at[tiles, 1 - core], inc.at[tiles], dev(xl, y, 1 - core, z, xh))

    def pair_add(copy, lo, n):
        copy.wait_recv()
        for t in range(lo, lo + n):
            inc[t] = inc[t] + acc[t, core]

    for x in range(2):
        for slot, xo in ((0, x), (1, 1 - x)):
            put(x * 2 + slot, tdot(ow[:, x * 256 : x * 256 + 256], o[:, xo * 256 : xo * 256 + 256]))
    pair0 = pair_sum(0, 4)
    forward(2)

    def x_send(k, lo):
        copies = []
        for dx in range(1, 4):
            xo, ho = xl ^ (dx % 2), xh ^ (dx // 2)
            copies.append(
                rdma(inc.at[pl.ds(lo + xo * 2, 2), :, ho], xin.at[k, me_x], dev(xo, y, core, z, ho))
            )
        return copies

    def x_sum(k, lo, copies):
        for c in copies:
            c.wait_recv()
        total = inc[pl.ds(lo + xl * 2, 2), :, xh]
        for dx in range(1, 4):
            total = total + xin[k, (xh ^ (dx // 2)) * 2 + (xl ^ (dx % 2))]
        xin[k, me_x] = total

    pair_add(pair0, 0, 4)
    x0 = x_send(0, 0)

    for c in gather:
        c.wait_recv()
    tf[...] = tg[0] + tg[1]

    def split(value):
        hi = value.astype(BF16).astype(F32)
        mid = (value - hi).astype(BF16).astype(F32)
        return hi, mid, value - hi - mid

    wide = lax.broadcasted_iota(jnp.int32, (128, 128), 0)
    pick = lax.broadcasted_iota(jnp.int32, (8, 128), 1) == (
        lax.broadcasted_iota(jnp.int32, (8, 128), 0) + af * 8
    )
    lanes = lax.broadcasted_iota(jnp.int32, (8, 128), 1).astype(F32)
    rows8 = []
    for k in range(9):
        j = (pa + k) % 16
        one, two = cls[0, pl.ds(j, 1), :], cls[1, pl.ds(j, 1), :]
        hot[:, k * 128 : (k + 1) * 128] = ((wide == one) | (wide == two)).astype(F32).astype(BF16)
        i = (pa + 16 - k) % 16
        ends = [
            jnp.sum(jnp.where(pick, cls[e, pl.ds(i, 1), :].astype(F32), 0.0), axis=1, keepdims=True) for e in range(2)
        ]
        rows8.append(((lanes == ends[0]) | (lanes == ends[1])).astype(F32))
    rows8.append(jnp.zeros((8, 128), F32))
    rows80 = jnp.concatenate(rows8, axis=0).astype(BF16)
    t8 = jnp.concatenate([*split(tf[pl.ds(pl.multiple_of(af * 8, 8), 8), :]), jnp.zeros((8, 128), F32)], axis=0)
    t8 = jnp.dot(t8.astype(BF16), hot[...], preferred_element_type=F32)
    own[...] = t8[0:8] + t8[8:16] + t8[16:24]
    others = sum(
        lax.dot_general(rows80, part.astype(BF16), (((1,), (1,)), ((), ())), preferred_element_type=F32)
        for part in split(tf[...])
    )
    for k in range(9):
        nsend[k] = others[k * 8 : (k + 1) * 8]
    oth[0] = nsend[0]

    forward(3)
    for x in range(2):
        put(4 + x * 4, tdot(ow[0:A, x * 256 : x * 256 + 256], ra[:, pl.ds(side(wrap(x, y == 3)), 256)]))
        put(6 + x * 4, tdot(ra[:, x * 256 : x * 256 + 256], ow[0:A, pl.ds(side(wrap(1 - x, y == 3)), 256)]))
        put(5 + x * 4, tdot(ow[A:KC, x * 256 : x * 256 + 256], rb[:, pl.ds(side(wrap(1 - x, y == 0)), 256)]))
        put(7 + x * 4, tdot(rb[:, x * 256 : x * 256 + 256], ow[A:KC, pl.ds(side(wrap(x, y == 0)), 256)]))
    pair1 = pair_sum(4, 8)

    x_sum(0, 0, x0)
    last = []
    for dz in range(1, 8):
        zo = (z + dz) % 8
        last.append(rdma(xin.at[0, me_x, :, zo], fin0.at[z], dev(xl, y, core, zo, xh)))
    fin0[z] = xin[0, me_x, :, z]

    flows = []
    for g in range(4):
        for way in (1, -1):
            steps = 3 if (g % 2 == 0) == (way == 1) else 4
            flows.append(dict(lo=4 + g * 2, way=way, steps=steps, target=up if way > 0 else down))

    def z_step(s):
        for f, flow in enumerate(flows):
            if s > flow["steps"]:
                continue
            if s:
                flow["copy"].wait_recv()
            if s == flow["steps"]:
                continue
            tiles = pl.ds(flow["lo"], 2)
            here = (z + flow["way"] * (flow["steps"] - s) + 16) % 8
            if s == 0:
                src = inc.at[tiles, here]
            else:
                src = zl.at[f, s - 1]
                src[...] = src[...] + inc[tiles, here]
            flow["copy"] = rdma(src, zl.at[f, s], flow["target"])

    pair_add(pair1, 4, 8)
    z_step(0)
    z_step(1)

    for p in range(4):
        for d in y_2[p]:
            d.wait_recv()
    at_a = pl.multiple_of(jnp.where(y < 2, 0, FA), 16)
    at_b = pl.multiple_of(A + jnp.where(y < 2, 0, FB), 16)
    for x in range(2):
        mine_x = side(wrap(x, y >= 2))
        other_x = side(wrap(x, y < 2))
        put(
            12 + x * 2,
            tdot(ow[pl.ds(at_a, FA), x * 256 : x * 256 + 256], fa[:, pl.ds(mine_x, 256)])
            + tdot(ow[pl.ds(at_b, FB), x * 256 : x * 256 + 256], fb[:, pl.ds(mine_x, 256)]),
        )
        put(
            13 + x * 2,
            tdot(fa[:, x * 256 : x * 256 + 256], ow[pl.ds(at_a, FA), pl.ds(other_x, 256)])
            + tdot(fb[:, x * 256 : x * 256 + 256], ow[pl.ds(at_b, FB), pl.ds(other_x, 256)]),
        )
    pair2 = pair_sum(12, 4)
    for k in range(1, 9):
        last.append(rdma(nsend.at[k], oth.at[k], {"pa": (pa + 16 - k) % 16, "af": af}))
    z_step(2)
    pair_add(pair2, 12, 4)
    x2 = x_send(1, 12)
    z_step(3)
    z_step(4)
    for g in range(4):
        lo = 4 + g * 2
        rz[g * 2 : g * 2 + 2] = (
            inc[lo : lo + 2, z] + zl[2 * g, flows[2 * g]["steps"] - 1] + zl[2 * g + 1, flows[2 * g + 1]["steps"] - 1]
        )
    for dx in range(4):
        xo, ho = xl ^ (dx % 2), xh ^ (dx // 2)
        base = xo * 4
        if dx:
            last.append(rdma(rz.at[pl.ds(base, 2), ho], fin1.at[me_x, 0:2], dev(xo, y, core, z, ho)))
        else:
            fin1[me_x, 0:2] = rz[pl.ds(base, 2), ho]
        for slot, yo in ((2, yp), (3, ym)):
            last.append(rdma(rz.at[base + slot, ho], fin1.at[me_x, slot], dev(xo, yo, core, z, ho)))

    x_sum(1, 12, x2)
    for dz in range(8):
        zo = (z + dz) % 8
        last.append(rdma(xin.at[1, me_x, 1, zo], fin2.at[z, 1], dev(xl, y2, core, zo, xh)))
        if dz:
            last.append(rdma(xin.at[1, me_x, 0, zo], fin2.at[z, 0], dev(xl, y, core, zo, xh)))
    fin2[z, 0] = xin[1, me_x, 0, z]
    for c in last:
        c.wait_recv()

    def total(parts):
        return functools.reduce(lambda p, q: p + q, parts)

    cross[:, 0:256] = total([fin0[s, 0] for s in range(8)])
    cross[:, 256:512] = total([fin1[s, t] for t in (0, 3) for s in range(4)])
    cross[:, 512:768] = total([fin2[s, t] for t in range(2) for s in range(8)])
    cross[:, 768:1024] = total([fin1[s, t] for t in (1, 2) for s in range(4)])
    cross[:, 1024:1280] = total([fin0[s, 1] for s in range(8)])
    shift = pl.multiple_of(core * 128, 128)
    for k in range(9):
        here = slice(k * 128, (k + 1) * 128)
        out_ref[:, here] = cross[:, pl.ds(pl.multiple_of(shift + k * 128, 128), 128)] / jnp.sqrt(
            own[:, here] * oth[k] + eps_norm
        )
    for c in started:
        c.wait_send()


def slopes(degrees):
    return jnp.tan(degrees.astype(F32) * (math.pi / 180.0))


def shards(spectra, tilt_min, tilt_max, tilt_axis):
    vmem = pl.BlockSpec(memory_space=pltpu.VMEM)
    scratch = [
        pltpu.VMEM((2, 2 * KC, 128), BF16),
        pltpu.VMEM((KC, 512), BF16),
        pltpu.VMEM((KC, 512), BF16),
        pltpu.VMEM((A, 512), BF16),
        pltpu.VMEM((B, 512), BF16),
        pltpu.VMEM((FA, 512), BF16),
        pltpu.VMEM((FB, 512), BF16),
        pltpu.VMEM((16, 2, 8, 2, 8, 256), F32),
        pltpu.VMEM((16, 8, 2, 8, 256), F32),
        pltpu.VMEM((2, 4, 2, 8, 8, 256), F32),
        pltpu.VMEM((8, 4, 2, 2, 8, 256), F32),
        pltpu.VMEM((8, 2, 8, 256), F32),
        pltpu.VMEM((8, 2, 8, 256), F32),
        pltpu.VMEM((4, 4, 8, 256), F32),
        pltpu.VMEM((8, 2, 8, 256), F32),
        pltpu.VMEM((2 * KC, 128), BF16),
        pltpu.VMEM((2 * KC, 128), BF16),
        pltpu.VMEM((128, 128), F32),
        pltpu.VMEM((2, 4, 16, 128), F32),
        pltpu.VMEM((2, 128, 128), F32),
        pltpu.VMEM((128, 128), F32),
        pltpu.VMEM((2, 16, 128), jnp.int32),
        pltpu.VMEM((128, 1152), BF16),
        pltpu.VMEM((8, 1152), F32),
        pltpu.VMEM((9, 8, 128), F32),
        pltpu.VMEM((9, 8, 128), F32),
        pltpu.VMEM((8, 1280), F32),
        pltpu.SemaphoreType.DMA((2,)),
        pltpu.SemaphoreType.DMA((N_SEM,)),
        pltpu.SemaphoreType.DMA((N_SEM,)),
    ]
    tilts = [t.reshape(16, 128) for t in (tilt_min, tilt_max, tilt_axis)]
    return pl.pallas_call(
        kernel,
        out_shape=jax.ShapeDtypeStruct((8, 1152), F32),
        in_specs=[pl.BlockSpec(memory_space=pl.ANY), vmem, vmem, vmem],
        out_specs=vmem,
        scratch_shapes=scratch,
        compiler_params=pltpu.CompilerParams(
            collective_id=0, has_side_effects=True, vmem_limit_bytes=56 * 2**20
        ),
    )(spectra, *tilts)


def solution(mesh):
    in_specs = (P(None, "af", "pa"), P(), P(), P())
    out_specs = P(("pa", "af"), None)
    return jax.shard_map(shards, mesh=mesh, in_specs=in_specs, out_specs=out_specs, check_vma=False)
```

time: 271 us -> 75 us (0.28)
  waiting for transfers between devices: 152 us -> 0 us
  matrix products: 15.7 us -> 0 us
  between operations: 13.6 us -> 0.01 us
  local copies, waits for them, and re-layouts: 6.47 us -> 1.39 us
  other arithmetic: 3.77 us -> 0 us
  Pallas kernels: 76.6 us -> 73.4 us
    psum x1 -> x0, waiting for transfers between devices: 152 us -> none  [shards(): table = lax.psum(table, 'af')]
    dot_general x3 -> x0, matrix products: 15.7 us -> none  [the longest x1 13.6 us: shards(): table = jnp.einsum('vi,vc->ic', power, c_keep, preferred_element_type=F32)]
    gather x2 -> x0, local copies, waits for them, and re-layouts: 6.37 us -> none  [the longest x1 3.66 us: shards(): other_norm = jnp.einsum('ic,jc->ij', h_own, table[band], precision=highest)]
    pallas_call x1, Pallas kernels: 76.6 us -> 73.4 us  [shards(): pl.pallas_call(kernel, out_shape=jax.ShapeDtypeStruct((8, 1152), F32), in...]
  transfers between devices with their start and end apart: 2 -> 0, of which waited for: 1 -> 0; matrix products, arithmetic and copies ran while one was open for 1% -> 0% of each run, Pallas kernels for 29% -> 0%
where the time goes in v2:
time: 75 us; the launch traced here: 74.8 us
  Pallas kernels  73.4 us (98%)
  local copies, waits for them, and re-layouts  1.39 us (2%)
    pallas_call x1, Pallas kernels, shards(): pl.pallas_call(kernel, out_shape=jax.ShapeDtypeStruct((8, 1152), F32), in...  73.4 us

profile of v2, /device:TPU:4, one launch (start us, length us, event | category | flops | bytes accessed | tf_op | source)
XLA Modules:
  0.0 74.8 jit_solution(12543684350050291994)
XLA Ops:
  0.0 73.4 %shard_map.46 = f32[8,1152]{1,0:T(8,128)} custom-call(bf16[2,3600,128]{2,1,0:T(8,128)(2,1)} %spec_hbm.1, s32[16,128]{1,0:T(8,128)} %bitcast.3, s32[16,128]{1,0:T(8,128)} %bitcast.4, s32[16,128]{1,0:T(8,128)} %bitcast.5), custom_call_target="tpu_custom_call" | custom-call | tf_op jit(solution)/shard_map/pallas_call | solution.py:486
  73.4 1.4 %copy.6 = f32[8,1152]{1,0:T(8,128)} copy(f32[8,1152]{1,0:T(8,128)} %shard_map.46) | data formatting | bytes 73728

commit v3 on v2

v3 whole, which is shorter than its diff:
```python
import functools
import math

import jax
import jax.numpy as jnp
from jax import lax
from jax.experimental import pallas as pl
from jax.experimental.pallas import tpu as pltpu
from jax.sharding import PartitionSpec as P

MESH = pl.DeviceIdType.MESH
F32 = jnp.float32
BF16 = jnp.bfloat16

G = 48
HALF = 25
VD = 3600
Q = 464
KC = 4 * Q
H1, H2 = 240, 224
A = 2 * Q + H1
B = 2 * Q + H2
MID = VD - KC
CHUNKS = ((0, 96), (96, 96), (192, 96), (288, 96), (384, 80))
T_LO, T_HI, N_T = 46, 70, 25
eps_norm = 1e-06


def coords():
    pa = lax.axis_index("pa")
    af = lax.axis_index("af")
    return pa // 8, (pa // 2) % 4, pa % 2, af // 2, af % 2


def dev(xl, y, core, z, xh):
    return {"pa": (xl * 4 + y) * 2 + core, "af": z * 2 + xh}


def tdot(lhs, rhs):
    return lax.dot_general(lhs, rhs, (((0,), (0,)), ((), ())), preferred_element_type=F32)


def cells(first, shape):
    v = (first + lax.broadcasted_iota(jnp.int32, shape, 0)).astype(F32)
    q = jnp.floor((v + 0.5) * (1.0 / HALF))
    iz = v - q * HALF
    ix = jnp.floor((q + 0.5) * (1.0 / G))
    iy = q - ix * G
    fx = jnp.where(ix < G // 2, ix, ix - G)
    fy = jnp.where(iy < G // 2, iy, iy - G)
    return fx, fy, iz

N_SEM = 176


def kernel(spec_hbm, tmin_ref, tmax_ref, axis_ref, out_ref, raw, m, wt, o, ow, ra, rb, rbw, acc, inc, xin0, xin1, xin2,
           zl, rz, fin0, fin1, fin2, fin3, pw, cm, tt, tl, tg, tf, cls, hot, own, nsend, oth, cross, load_sem, ssem, rsem):
    xl, y, core, z, xh = coords()
    pa = lax.axis_index("pa")
    af = lax.axis_index("af")
    yp, ym = (y + 1) % 4, (y + 3) % 4
    zp, zm = (z + 1) % 8, (z + 7) % 8
    me_x = xh * 2 + xl
    started = []

    def rdma(src, dst, target):
        i = len(started)
        c = pltpu.make_async_remote_copy(
            src_ref=src, dst_ref=dst, send_sem=ssem.at[i], recv_sem=rsem.at[i], device_id=target, device_id_type=MESH
        )
        c.start()
        started.append(c)
        return c

    loads = []
    for first, n in ((core * KC, MID), (MID, KC - MID), ((1 - core) * KC, MID)):
        here = pl.ds(first if isinstance(first, int) else pl.multiple_of(first, 16), n)
        for p in range(2):
            c = pltpu.make_async_copy(spec_hbm.at[p, here], raw.at[p, here], load_sem.at[len(loads)])
            c.start()
            loads.append(c)
    barrier = pltpu.get_barrier_semaphore()
    peers = [
        dev(xl, y, 1 - core, z, xh),
        dev(1 - xl, y, core, z, xh),
        dev(1 - xl, y, 1 - core, z, xh),
        dev(xl, yp, core, z, xh),
        dev(xl, ym, core, z, xh),
        dev(xl, y, core, z, 1 - xh),
        dev(xl, y, core, zp, xh),
        dev(xl, y, core, zm, xh),
    ]
    for peer in peers:
        pl.semaphore_signal(barrier, inc=1, device_id=peer, device_id_type=MESH)
    raw[:, VD:, :] = jnp.zeros((2, 2 * KC - VD, 128), BF16)

    cls[0] = axis_ref[...] * 50 + (-T_LO - tmin_ref[...])
    cls[1] = axis_ref[...] * 50 + (N_T - T_LO + tmax_ref[...])
    lower = slopes(tmin_ref[pl.ds(pa, 1), :])
    upper = slopes(tmax_ref[pl.ds(pa, 1), :])
    axis = axis_ref[pl.ds(pa, 1), :]
    lane = lax.broadcasted_iota(jnp.int32, (1, 128), 1)
    c_axis = (lane >= 50).astype(jnp.int32)
    c_side = ((lane - c_axis * 50) >= 25).astype(jnp.int32)
    c_slope = slopes(lane - c_axis * 50 - c_side * 25 + T_LO)
    c_slope = jnp.where(lane < 100, c_slope, -1.0)

    def own_col(dx, dc):
        return pl.multiple_of(((xl ^ dx) * 2 + (core ^ dc)) * 128, 128)

    def by_chunk(half, body):
        def slot(s, carry):
            first = half * KC + (y + 3 - s) % 4 * Q
            for r0, n in CHUNKS:
                body(pl.multiple_of(first + r0, 16), pl.ds(pl.multiple_of(s * Q + r0, 16), n), n)
            return carry

        lax.fori_loop(0, 4, slot, 0)

    def mask_half(half):
        def body(r0, to, n):
            fx, fy, iz = cells(af * VD + r0, (n, 128))
            u = jnp.where(axis == 1, fx, fy)
            a = jnp.abs(u)
            b = jnp.where(u >= 0.0, -iz, iz)
            keep = ((a * lower <= b) & (b <= a * upper)).astype(F32)
            for p in range(2):
                m[p, half, to, :] = (raw[p, pl.ds(r0, n), :].astype(F32) * keep).astype(BF16)

        by_chunk(half, body)

    for c in loads[:4]:
        c.wait()
    mask_half(core)
    pl.semaphore_wait(barrier, len(peers))

    col = own_col(0, 0)
    o[:, pl.ds(col, 128)] = m[xl, core]

    y1 = [[] for _ in range(4)]

    def to_minus(p, r0, n):
        c = pl.ds(own_col(p // 2, p % 2), 128)
        y1[p].append(rdma(o.at[pl.ds(r0, n), c], ra.at[pl.ds(r0 - Q, n), c], dev(xl, ym, core, z, xh)))

    def to_plus(p, r0, n, to):
        c = pl.ds(own_col(p // 2, p % 2), 128)
        y1[p].append(rdma(o.at[pl.ds(r0, n), c], rb.at[pl.ds(to, n), c], dev(xl, yp, core, z, xh)))

    def y_send(p):
        to_plus(p, 3 * Q, Q, 0)
        to_minus(p, Q, A)
        to_plus(p, 0, Q, Q)
        to_plus(p, 2 * Q + H1, H2, 2 * Q)

    def to_x(half, r0, n, target):
        return rdma(m.at[1 - xl, half, pl.ds(r0, n)], o.at[pl.ds(r0, n), pl.ds(col, 128)], target)

    y_send(0)
    x_same = [to_x(core, r0, 2 * Q, dev(1 - xl, y, core, z, xh)) for r0 in (2 * Q, 0)]
    for c in loads[4:]:
        c.wait()
    mask_half(1 - core)
    sib = rdma(m.at[xl, 1 - core], o.at[:, pl.ds(col, 128)], dev(xl, y, 1 - core, z, xh))
    x_other = [to_x(1 - core, q * Q, Q, dev(1 - xl, y, 1 - core, z, xh)) for q in (3, 2, 0, 1)]

    for half in range(2):

        def powers(r0, to, n, half=half):
            fx, fy, iz = cells(af * VD + r0, (n, 128))
            re = m[0, half, to, :].astype(F32)
            im = m[1, half, to, :].astype(F32)
            w = jnp.where((iz < 0.5) | (iz > 23.5), 1.0, 2.0)
            pw[half, to, :] = (w * (re * re + im * im)).astype(BF16)
            u = jnp.where(c_axis == 1, fx, fy)
            side = (u < 0.0).astype(jnp.int32)
            keep = (iz <= jnp.abs(u) * c_slope) & (side == c_side) & (lane < 100)
            cm[half, to, :] = keep.astype(F32).astype(BF16)

        by_chunk(half, powers)
    tt[...] = tdot(pw[0], cm[0]) + tdot(pw[1], cm[1])

    def rows16(zz):
        return pl.ds(pl.multiple_of(((zz + 16) % 8) * 16, 16), 16)

    up, down = dev(xl, y, core, zp, xh), dev(xl, y, core, zm, xh)
    t_flows = [dict(way=1, steps=3, target=up), dict(way=-1, steps=4, target=down)]

    def t_step(s):
        for f, flow in enumerate(t_flows):
            if s > flow["steps"]:
                continue
            if s:
                flow["copy"].wait_recv()
            if s == flow["steps"]:
                continue
            here = rows16(z + flow["way"] * (flow["steps"] - s))
            if s == 0:
                src = tt.at[here]
            else:
                src = tl.at[f, s - 1]
                src[...] = src[...] + tt[here, :]
            flow["copy"] = rdma(src, tl.at[f, s], flow["target"])

    t_step(0)

    def weights(r0, to, n):
        iz = cells(af * VD + r0, (n, 128))[2]
        wt[to, :] = jnp.where((iz < 0.5) | (iz > 23.5), 1.0, 2.0).astype(BF16)

    by_chunk(core, weights)

    def weigh(dst, src, x, n):
        for dc in range(2):
            here = pl.ds(pl.multiple_of(x * 256 + dc * 128, 128), 128)
            dst[:, here] = src[0:n, here] * wt[0:n, :]

    sib.wait_recv()
    y_send(1)
    t_step(1)
    weigh(ow, o, xl, KC)
    t_step(2)
    x_same[0].wait_recv()
    to_plus(2, 3 * Q, Q, 0)
    to_minus(2, 2 * Q, Q + H1)
    to_plus(2, 2 * Q + H1, H2, 2 * Q)
    t_step(3)
    x_same[1].wait_recv()
    to_plus(2, 0, Q, Q)
    to_minus(2, Q, Q)
    t_step(4)
    mine16 = rows16(z)
    tg[xh, mine16, :] = tt[mine16, :] + tl[0, 2] + tl[1, 3]
    gather = []
    for dz in range(8):
        for dh in range(2):
            if dz or dh:
                part = tg.at[xh, mine16]
                gather.append(rdma(part, part, dev(xl, y, core, (z + dz) % 8, xh ^ dh)))

    x_other[0].wait_recv()
    to_plus(3, 3 * Q, Q, 0)
    to_minus(3, 3 * Q, H1)
    x_other[1].wait_recv()
    to_plus(3, 2 * Q + H1, H2, 2 * Q)
    to_minus(3, 2 * Q, Q)
    for p in range(2):
        for d in y1[p]:
            d.wait_recv()
    weigh(rbw, rb, xl, 2 * Q)
    x_other[2].wait_recv()
    to_plus(3, 0, Q, Q)
    x_other[3].wait_recv()
    to_minus(3, Q, Q)
    weigh(ow, o, 1 - xl, KC)

    def put(tile, value):
        acc[tile] = value.reshape(2, 8, 2, 8, 256)

    def side(x):
        return pl.multiple_of(x * 256, 256)

    def wrap(x, cond):
        return x ^ cond.astype(jnp.int32)

    def pair_sum(lo, n):
        tiles = pl.ds(lo, n)
        return rdma(acc.at[tiles, 1 - core], inc.at[tiles], dev(xl, y, 1 - core, z, xh))

    def pair_add(copy, lo, n):
        copy.wait_recv()
        for t in range(lo, lo + n):
            inc[t] = inc[t] + acc[t, core]

    for x in range(2):
        for slot, xo in ((0, x), (1, 1 - x)):
            put(x * 2 + slot, tdot(ow[:, x * 256 : x * 256 + 256], o[:, xo * 256 : xo * 256 + 256]))
    pair0 = pair_sum(0, 4)

    def x_send(lo, n, buf):
        copies = []
        for dx in range(1, 4):
            xo, ho = xl ^ (dx % 2), xh ^ (dx // 2)
            copies.append(
                rdma(inc.at[pl.ds(lo + xo * n, n), :, ho], buf.at[me_x], dev(xo, y, core, z, ho))
            )
        return copies

    def x_sum(lo, n, buf, copies):
        for c in copies:
            c.wait_recv()
        total = inc[pl.ds(lo + xl * n, n), :, xh]
        for dx in range(1, 4):
            total = total + buf[(xh ^ (dx // 2)) * 2 + (xl ^ (dx % 2))]
        buf[me_x] = total

    pair_add(pair0, 0, 4)
    x0 = x_send(0, 2, xin0)

    for c in gather:
        c.wait_recv()
    tf[...] = tg[0] + tg[1]

    def split(value):
        hi = value.astype(BF16).astype(F32)
        mid = (value - hi).astype(BF16).astype(F32)
        return hi, mid, value - hi - mid

    wide = lax.broadcasted_iota(jnp.int32, (128, 128), 0)
    pick = lax.broadcasted_iota(jnp.int32, (8, 128), 1) == (
        lax.broadcasted_iota(jnp.int32, (8, 128), 0) + af * 8
    )
    lanes = lax.broadcasted_iota(jnp.int32, (8, 128), 1).astype(F32)
    rows8 = []
    for k in range(9):
        j = (pa + k) % 16
        one, two = cls[0, pl.ds(j, 1), :], cls[1, pl.ds(j, 1), :]
        hot[:, k * 128 : (k + 1) * 128] = ((wide == one) | (wide == two)).astype(F32).astype(BF16)
        i = (pa + 16 - k) % 16
        ends = [
            jnp.sum(jnp.where(pick, cls[e, pl.ds(i, 1), :].astype(F32), 0.0), axis=1, keepdims=True) for e in range(2)
        ]
        rows8.append(((lanes == ends[0]) | (lanes == ends[1])).astype(F32))
    rows8.append(jnp.zeros((8, 128), F32))
    rows80 = jnp.concatenate(rows8, axis=0).astype(BF16)
    t8 = jnp.concatenate([*split(tf[pl.ds(pl.multiple_of(af * 8, 8), 8), :]), jnp.zeros((8, 128), F32)], axis=0)
    t8 = jnp.dot(t8.astype(BF16), hot[...], preferred_element_type=F32)
    own[...] = t8[0:8] + t8[8:16] + t8[16:24]
    others = sum(
        lax.dot_general(rows80, part.astype(BF16), (((1,), (1,)), ((), ())), preferred_element_type=F32)
        for part in split(tf[...])
    )
    for k in range(9):
        nsend[k] = others[k * 8 : (k + 1) * 8]
    oth[0] = nsend[0]

    for p in range(2, 4):
        for d in y1[p]:
            d.wait_recv()
    weigh(rbw, rb, 1 - xl, 2 * Q)

    def cols(ref, x, first, n):
        return ref[first : first + n, pl.ds(side(x), 256)]

    for x in range(2):
        put(4 + x, tdot(cols(ow, x, 0, A), cols(ra, wrap(x, y == 3), 0, A)))
        put(6 + x, tdot(cols(ra, x, 0, A), cols(ow, wrap(1 - x, y == 3), 0, A)))
    pair1 = pair_sum(4, 4)
    for x in range(2):
        put(
            8 + x,
            tdot(cols(ow, x, 0, Q), cols(rb, wrap(1 - x, y == 0), 0, Q))
            + tdot(cols(ow, x, 3 * Q + H1, H2), cols(rb, wrap(1 - x, y == 0), 2 * Q, H2)),
        )
        put(
            10 + x,
            tdot(cols(rb, x, 0, Q), cols(ow, wrap(x, y == 0), 0, Q))
            + tdot(cols(rb, x, 2 * Q, H2), cols(ow, wrap(x, y == 0), 3 * Q + H1, H2)),
        )
    pair2 = pair_sum(8, 4)

    flows = []
    for g in range(3):
        for way in (1, -1):
            steps = 3 if (g % 2 == 0) == (way == 1) else 4
            flows.append(dict(lo=4 + g * 2, way=way, steps=steps, target=up if way > 0 else down))

    def z_step(s, which=(0, 6)):
        for f, flow in list(enumerate(flows))[which[0] : which[1]]:
            if s > flow["steps"]:
                continue
            if s:
                flow["copy"].wait_recv()
            if s == flow["steps"]:
                continue
            tiles = pl.ds(flow["lo"], 2)
            here = (z + flow["way"] * (flow["steps"] - s) + 16) % 8
            if s == 0:
                src = inc.at[tiles, here]
            else:
                src = zl.at[f, s - 1]
                src[...] = src[...] + inc[tiles, here]
            flow["copy"] = rdma(src, zl.at[f, s], flow["target"])

    pair_add(pair1, 4, 4)
    z_step(0, (0, 4))
    for x in range(2):
        put(12 + x * 2, tdot(cols(rbw, x, 0, 2 * Q), cols(ra, wrap(x, ym >= 2), 0, 2 * Q)))
        put(13 + x * 2, tdot(cols(ra, x, 0, 2 * Q), cols(rbw, wrap(x, yp >= 2), 0, 2 * Q)))
    pair3 = pair_sum(12, 4)
    pair_add(pair2, 8, 4)
    z_step(0, (4, 6))
    x1 = x_send(10, 1, xin1)
    x_sum(0, 2, xin0, x0)
    last = []
    for dz in range(1, 8):
        zo = (z + dz) % 8
        last.append(rdma(xin0.at[me_x, :, zo], fin0.at[z], dev(xl, y, core, zo, xh)))
    fin0[z] = xin0[me_x, :, z]
    pair_add(pair3, 12, 4)
    x2 = x_send(12, 2, xin2)
    z_step(1)
    for k in range(1, 9):
        last.append(rdma(nsend.at[k], oth.at[k], {"pa": (pa + 16 - k) % 16, "af": af}))
    x_sum(10, 1, xin1, x1)
    for dz in range(8):
        zo = (z + dz) % 8
        last.append(rdma(xin1.at[me_x, 0, zo], fin1.at[z], dev(xl, ym, core, zo, xh)))
    z_step(2)
    x_sum(12, 2, xin2, x2)
    for dz in range(8):
        zo = (z + dz) % 8
        last.append(rdma(xin2.at[me_x, 0, zo], fin2.at[z, 0], dev(xl, ym, core, zo, xh)))
        last.append(rdma(xin2.at[me_x, 1, zo], fin2.at[z, 1], dev(xl, yp, core, zo, xh)))
    z_step(3)
    z_step(4)
    for g in range(3):
        lo = 4 + g * 2
        rz[lo - 4 : lo - 2] = (
            inc[lo : lo + 2, z] + zl[2 * g, flows[2 * g]["steps"] - 1] + zl[2 * g + 1, flows[2 * g + 1]["steps"] - 1]
        )
    for dx in range(4):
        xo, ho = xl ^ (dx % 2), xh ^ (dx // 2)
        for slot in range(3):
            if slot == 1:
                last.append(rdma(rz.at[2 + xo, ho], fin3.at[me_x, 1], dev(xo, yp, core, z, ho)))
            elif dx:
                last.append(rdma(rz.at[2 * slot + xo, ho], fin3.at[me_x, slot], dev(xo, y, core, z, ho)))
            else:
                fin3[me_x, slot] = rz[2 * slot + xo, ho]
    for c in last:
        c.wait_recv()

    def total(parts):
        return functools.reduce(lambda p, q: p + q, parts)

    cross[:, 0:256] = total([fin0[s, 0] for s in range(8)])
    cross[:, 256:512] = total([fin1[s] for s in range(8)] + [fin3[s, 0] for s in range(4)])
    cross[:, 512:768] = total([fin2[s, t] for t in range(2) for s in range(8)])
    cross[:, 768:1024] = total([fin3[s, t] for t in (1, 2) for s in range(4)])
    cross[:, 1024:1280] = total([fin0[s, 1] for s in range(8)])
    shift = pl.multiple_of(core * 128, 128)
    for k in range(9):
        here = slice(k * 128, (k + 1) * 128)
        out_ref[:, here] = cross[:, pl.ds(pl.multiple_of(shift + k * 128, 128), 128)] / jnp.sqrt(
            own[:, here] * oth[k] + eps_norm
        )
    for c in started:
        c.wait_send()


def slopes(degrees):
    return jnp.tan(degrees.astype(F32) * (math.pi / 180.0))


def shards(spectra, tilt_min, tilt_max, tilt_axis):
    vmem = pl.BlockSpec(memory_space=pltpu.VMEM)
    scratch = [
        pltpu.VMEM((2, 2 * KC, 128), BF16),
        pltpu.VMEM((2, 2, KC, 128), BF16),
        pltpu.VMEM((KC, 128), BF16),
        pltpu.VMEM((KC, 512), BF16),
        pltpu.VMEM((KC, 512), BF16),
        pltpu.VMEM((A, 512), BF16),
        pltpu.VMEM((B, 512), BF16),
        pltpu.VMEM((2 * Q, 512), BF16),
        pltpu.VMEM((16, 2, 8, 2, 8, 256), F32),
        pltpu.VMEM((16, 8, 2, 8, 256), F32),
        pltpu.VMEM((4, 2, 8, 8, 256), F32),
        pltpu.VMEM((4, 1, 8, 8, 256), F32),
        pltpu.VMEM((4, 2, 8, 8, 256), F32),
        pltpu.VMEM((6, 4, 2, 2, 8, 256), F32),
        pltpu.VMEM((6, 2, 8, 256), F32),
        pltpu.VMEM((8, 2, 8, 256), F32),
        pltpu.VMEM((8, 8, 256), F32),
        pltpu.VMEM((8, 2, 8, 256), F32),
        pltpu.VMEM((4, 3, 8, 256), F32),
        pltpu.VMEM((2, KC, 128), BF16),
        pltpu.VMEM((2, KC, 128), BF16),
        pltpu.VMEM((128, 128), F32),
        pltpu.VMEM((2, 4, 16, 128), F32),
        pltpu.VMEM((2, 128, 128), F32),
        pltpu.VMEM((128, 128), F32),
        pltpu.VMEM((2, 16, 128), jnp.int32),
        pltpu.VMEM((128, 1152), BF16),
        pltpu.VMEM((8, 1152), F32),
        pltpu.VMEM((9, 8, 128), F32),
        pltpu.VMEM((9, 8, 128), F32),
        pltpu.VMEM((8, 1280), F32),
        pltpu.SemaphoreType.DMA((6,)),
        pltpu.SemaphoreType.DMA((N_SEM,)),
        pltpu.SemaphoreType.DMA((N_SEM,)),
    ]
    tilts = [t.reshape(16, 128) for t in (tilt_min, tilt_max, tilt_axis)]
    return pl.pallas_call(
        kernel,
        out_shape=jax.ShapeDtypeStruct((8, 1152), F32),
        in_specs=[pl.BlockSpec(memory_space=pl.ANY), vmem, vmem, vmem],
        out_specs=vmem,
        scratch_shapes=scratch,
        compiler_params=pltpu.CompilerParams(
            collective_id=0, has_side_effects=True, vmem_limit_bytes=56 * 2**20
        ),
    )(spectra, *tilts)


def solution(mesh):
    in_specs = (P(None, "af", "pa"), P(), P(), P())
    out_specs = P(("pa", "af"), None)
    return jax.shard_map(shards, mesh=mesh, in_specs=in_specs, out_specs=out_specs, check_vma=False)
```

time: 75 us -> 67.7 us (0.903)
  Pallas kernels: 73.4 us -> 66.1 us
    pallas_call x1, Pallas kernels: 73.4 us -> 66.1 us  [shards(): pl.pallas_call(kernel, out_shape=jax.ShapeDtypeStruct((8, 1152), F32), in...]
where the time goes in v3:
time: 67.7 us; the launch traced here: 67.5 us
  Pallas kernels  66.1 us (98%)
  local copies, waits for them, and re-layouts  1.39 us (2%)
    pallas_call x1, Pallas kernels, shards(): pl.pallas_call(kernel, out_shape=jax.ShapeDtypeStruct((8, 1152), F32), in...  66.1 us
    unnamed x1, local copies, waits for them, and re-layouts  1.39 us

profile of v3, /device:TPU:4, one launch (start us, length us, event | category | flops | bytes accessed | tf_op | source)
XLA Modules:
  0.0 67.5 jit_solution(17281673427191722749)
XLA Ops:
  0.0 66.1 %shard_map.46 = f32[8,1152]{1,0:T(8,128)} custom-call(bf16[2,3600,128]{2,1,0:T(8,128)(2,1)} %spec_hbm.1, s32[16,128]{1,0:T(8,128)} %bitcast.3, s32[16,128]{1,0:T(8,128)} %bitcast.4, s32[16,128]{1,0:T(8,128)} %bitcast.5), custom_call_target="tpu_custom_call" | custom-call | tf_op jit(solution)/shard_map/pallas_call | solution.py:495
  66.1 1.4 %copy.6 = f32[8,1152]{1,0:T(8,128)} copy(f32[8,1152]{1,0:T(8,128)} %shard_map.46) | data formatting | bytes 73728

commit v4 on v3

--- a/solution.py
+++ b/solution.py
@@ -50,10 +50,10 @@
     fy = jnp.where(iy < G // 2, iy, iy - G)
     return fx, fy, iz
 
-N_SEM = 176
-
-
-def kernel(spec_hbm, tmin_ref, tmax_ref, axis_ref, out_ref, raw, m, wt, o, ow, ra, rb, rbw, acc, inc, xin0, xin1, xin2,
+N_SEM = 256
+
+
+def kernel(spec_hbm, tmin_hbm, tmax_hbm, axis_hbm, out_ref, tilt, raw, m, wt, o, ow, ra, rb, rbw, acc, inc, xin0, xin2,
            zl, rz, fin0, fin1, fin2, fin3, pw, cm, tt, tl, tg, tf, cls, hot, own, nsend, oth, cross, load_sem, ssem, rsem):
     xl, y, core, z, xh = coords()
     pa = lax.axis_index("pa")
@@ -73,6 +73,11 @@
         return c
 
     loads = []
+    for i, ref in enumerate((tmin_hbm, tmax_hbm, axis_hbm)):
+        c = pltpu.make_async_copy(ref, tilt.at[i], load_sem.at[i])
+        c.start()
+        loads.append(c)
+    tmin_ref, tmax_ref, axis_ref = tilt.at[0], tilt.at[1], tilt.at[2]
     for first, n in ((core * KC, MID), (MID, KC - MID), ((1 - core) * KC, MID)):
         here = pl.ds(first if isinstance(first, int) else pl.multiple_of(first, 16), n)
         for p in range(2):
@@ -94,6 +99,8 @@
         pl.semaphore_signal(barrier, inc=1, device_id=peer, device_id_type=MESH)
     raw[:, VD:, :] = jnp.zeros((2, 2 * KC - VD, 128), BF16)
 
+    for c in loads[:3]:
+        c.wait()
     cls[0] = axis_ref[...] * 50 + (-T_LO - tmin_ref[...])
     cls[1] = axis_ref[...] * 50 + (N_T - T_LO + tmax_ref[...])
     lower = slopes(tmin_ref[pl.ds(pa, 1), :])
@@ -108,16 +115,16 @@
     def own_col(dx, dc):
         return pl.multiple_of(((xl ^ dx) * 2 + (core ^ dc)) * 128, 128)
 
-    def by_chunk(half, body):
+    def by_chunk(half, body, slots=(0, 4)):
         def slot(s, carry):
             first = half * KC + (y + 3 - s) % 4 * Q
             for r0, n in CHUNKS:
                 body(pl.multiple_of(first + r0, 16), pl.ds(pl.multiple_of(s * Q + r0, 16), n), n)
             return carry
 
-        lax.fori_loop(0, 4, slot, 0)
-
-    def mask_half(half):
+        lax.fori_loop(*slots, slot, 0)
+
+    def mask_half(half, slots=(0, 4)):
         def body(r0, to, n):
             fx, fy, iz = cells(af * VD + r0, (n, 128))
             u = jnp.where(axis == 1, fx, fy)
@@ -127,15 +134,14 @@
             for p in range(2):
                 m[p, half, to, :] = (raw[p, pl.ds(r0, n), :].astype(F32) * keep).astype(BF16)
 
-        by_chunk(half, body)
-
-    for c in loads[:4]:
+        by_chunk(half, body, slots)
+
+    for c in loads[3:7]:
         c.wait()
-    mask_half(core)
+    mask_half(core, (2, 4))
     pl.semaphore_wait(barrier, len(peers))
 
     col = own_col(0, 0)
-    o[:, pl.ds(col, 128)] = m[xl, core]
 
     y1 = [[] for _ in range(4)]
 
@@ -147,18 +153,27 @@
         c = pl.ds(own_col(p // 2, p % 2), 128)
         y1[p].append(rdma(o.at[pl.ds(r0, n), c], rb.at[pl.ds(to, n), c], dev(xl, yp, core, z, xh)))
 
-    def y_send(p):
+    def y_high(p):
         to_plus(p, 3 * Q, Q, 0)
-        to_minus(p, Q, A)
+        to_minus(p, 2 * Q, Q + H1)
+        to_plus(p, 2 * Q + H1, H2, 2 * Q)
+
+    def y_low(p):
         to_plus(p, 0, Q, Q)
-        to_plus(p, 2 * Q + H1, H2, 2 * Q)
+        to_minus(p, Q, Q)
 
     def to_x(half, r0, n, target):
         return rdma(m.at[1 - xl, half, pl.ds(r0, n)], o.at[pl.ds(r0, n), pl.ds(col, 128)], target)
 
-    y_send(0)
-    x_same = [to_x(core, r0, 2 * Q, dev(1 - xl, y, core, z, xh)) for r0 in (2 * Q, 0)]
-    for c in loads[4:]:
+    own_high, own_low = pl.ds(2 * Q, 2 * Q), pl.ds(0, 2 * Q)
+    x_same = [to_x(core, 2 * Q, 2 * Q, dev(1 - xl, y, core, z, xh))]
+    o[own_high, pl.ds(col, 128)] = m[xl, core, own_high]
+    y_high(0)
+    mask_half(core, (0, 2))
+    x_same.append(to_x(core, 0, 2 * Q, dev(1 - xl, y, core, z, xh)))
+    o[own_low, pl.ds(col, 128)] = m[xl, core, own_low]
+    y_low(0)
+    for c in loads[7:]:
         c.wait()
     mask_half(1 - core)
     sib = rdma(m.at[xl, 1 - core], o.at[:, pl.ds(col, 128)], dev(xl, y, 1 - core, z, xh))
@@ -178,6 +193,10 @@
             cm[half, to, :] = keep.astype(F32).astype(BF16)
 
         by_chunk(half, powers)
+        if half == 0:
+            sib.wait_recv()
+            y_high(1)
+            y_low(1)
     tt[...] = tdot(pw[0], cm[0]) + tdot(pw[1], cm[1])
 
     def rows16(zz):
@@ -215,19 +234,20 @@
             here = pl.ds(pl.multiple_of(x * 256 + dc * 128, 128), 128)
             dst[:, here] = src[0:n, here] * wt[0:n, :]
 
-    sib.wait_recv()
-    y_send(1)
+    x_same[0].wait_recv()
+    y_high(2)
     t_step(1)
     weigh(ow, o, xl, KC)
+    x_same[1].wait_recv()
+    y_low(2)
     t_step(2)
-    x_same[0].wait_recv()
-    to_plus(2, 3 * Q, Q, 0)
-    to_minus(2, 2 * Q, Q + H1)
-    to_plus(2, 2 * Q + H1, H2, 2 * Q)
+    x_other[0].wait_recv()
+    to_plus(3, 3 * Q, Q, 0)
+    to_minus(3, 3 * Q, H1)
     t_step(3)
-    x_same[1].wait_recv()
-    to_plus(2, 0, Q, Q)
-    to_minus(2, Q, Q)
+    x_other[1].wait_recv()
+    to_plus(3, 2 * Q + H1, H2, 2 * Q)
+    to_minus(3, 2 * Q, Q)
     t_step(4)
     mine16 = rows16(z)
     tg[xh, mine16, :] = tt[mine16, :] + tl[0, 2] + tl[1, 3]
@@ -238,16 +258,6 @@
                 part = tg.at[xh, mine16]
                 gather.append(rdma(part, part, dev(xl, y, core, (z + dz) % 8, xh ^ dh)))
 
-    x_other[0].wait_recv()
-    to_plus(3, 3 * Q, Q, 0)
-    to_minus(3, 3 * Q, H1)
-    x_other[1].wait_recv()
-    to_plus(3, 2 * Q + H1, H2, 2 * Q)
-    to_minus(3, 2 * Q, Q)
-    for p in range(2):
-        for d in y1[p]:
-            d.wait_recv()
-    weigh(rbw, rb, xl, 2 * Q)
     x_other[2].wait_recv()
     to_plus(3, 0, Q, Q)
     x_other[3].wait_recv()
@@ -294,8 +304,121 @@
             total = total + buf[(xh ^ (dx // 2)) * 2 + (xl ^ (dx % 2))]
         buf[me_x] = total
 
+    def cols(ref, x, first, n):
+        return ref[first : first + n, pl.ds(side(x), 256)]
+
+    early = (wrap(xl, y == 3), xl, wrap(1 - xl, y == 0), xl)
+
+    def kinds(lo, late):
+        x0, x1, x2, x3 = (x ^ late for x in early)
+        xr = xl ^ late
+        put(lo, tdot(cols(ow, x0, 0, A), cols(ra, xr, 0, A)))
+        put(lo + 1, tdot(cols(ra, x1, 0, A), cols(ow, wrap(1 - x1, y == 3), 0, A)))
+        put(
+            lo + 2,
+            tdot(cols(ow, x2, 0, Q), cols(rb, xr, 0, Q))
+            + tdot(cols(ow, x2, 3 * Q + H1, H2), cols(rb, xr, 2 * Q, H2)),
+        )
+        put(
+            lo + 3,
+            tdot(cols(rb, x3, 0, Q), cols(ow, wrap(x3, y == 0), 0, Q))
+            + tdot(cols(rb, x3, 2 * Q, H2), cols(ow, wrap(x3, y == 0), 3 * Q + H1, H2)),
+        )
+        return pair_sum(lo, 4)
+
+    for p in range(2):
+        for d in y1[p]:
+            d.wait_recv()
+    pair1 = kinds(4, 0)
+    weigh(rbw, rb, xl, 2 * Q)
     pair_add(pair0, 0, 4)
     x0 = x_send(0, 2, xin0)
+
+    owners = (y, yp, y, ym)
+    last = []
+    flows = []
+    for g in range(4):
+        for way in (1, -1):
+            flows.append(
+                dict(
+                    lo=4 + g * 2,
+                    way=way,
+                    far=(g % 2 == 0) == (way == -1),
+                    near=up if way > 0 else down,
+                    second=dev(xl, y, core, (z + 2 * way + 8) % 8, xh),
+                )
+            )
+    early_flows, late_flows = (0, 4), (4, 8)
+
+    def z_step(s, which):
+        for f, flow in list(enumerate(flows))[which[0] : which[1]]:
+            tiles, way = pl.ds(flow["lo"], 2), flow["way"]
+
+            def rows_for(d, way=way):
+                return (z + way * d + 8) % 8
+
+            if s == 0:
+                flow["copy"] = rdma(inc.at[tiles, rows_for(3)], zl.at[f, 0], flow["near"])
+                if flow["far"]:
+                    flow["copy2"] = rdma(inc.at[tiles, rows_for(4)], zl.at[f, 1], flow["second"])
+            elif s == 1:
+                flow["copy"].wait_recv()
+                value = zl[f, 0] + inc[tiles, rows_for(2)]
+                if flow["far"]:
+                    flow["copy2"].wait_recv()
+                    value = value + zl[f, 1]
+                zl[f, 0] = value
+                flow["copy"] = rdma(zl.at[f, 0], zl.at[f, 2], flow["near"])
+            else:
+                flow["copy"].wait_recv()
+                zl[f, 2] = zl[f, 2] + inc[tiles, rows_for(1)]
+                for i in range(2):
+                    kind, late = (flow["lo"] + i) % 4, f // 4
+                    for ho in (xh, 1 - xh):
+                        last.append(
+                            rdma(
+                                zl.at[f, 2, i, ho],
+                                fin1.at[(1 - way) // 2, me_x, kind],
+                                dev(early[kind] ^ late, owners[kind], core, rows_for(1), ho),
+                            )
+                        )
+
+    def own_rows():
+        for kind in range(4):
+            rz[kind * 2 + early[kind]] = inc[4 + kind, z]
+            rz[kind * 2 + (early[kind] ^ 1)] = inc[8 + kind, z]
+        for dx in range(4):
+            xo, ho = xl ^ (dx % 2), xh ^ (dx // 2)
+            for kind, yo in enumerate(owners):
+                if dx or kind % 2:
+                    last.append(rdma(rz.at[2 * kind + xo, ho], fin3.at[me_x, kind], dev(xo, yo, core, z, ho)))
+                else:
+                    fin3[me_x, kind] = rz[2 * kind + xo, ho]
+
+    pair_add(pair1, 4, 4)
+    z_step(0, early_flows)
+    for p in range(2, 4):
+        for d in y1[p]:
+            d.wait_recv()
+    weigh(rbw, rb, 1 - xl, 2 * Q)
+    for x in range(2):
+        put(12 + x * 2, tdot(cols(rbw, x, 0, 2 * Q), cols(ra, wrap(x, ym >= 2), 0, 2 * Q)))
+        put(13 + x * 2, tdot(cols(ra, x, 0, 2 * Q), cols(rbw, wrap(x, yp >= 2), 0, 2 * Q)))
+    pair3 = pair_sum(12, 4)
+    pair2 = kinds(8, 1)
+    pair_add(pair3, 12, 4)
+    x2 = x_send(12, 2, xin2)
+    pair_add(pair2, 8, 4)
+    z_step(0, late_flows)
+    z_step(1, early_flows)
+    own_rows()
+    x_sum(0, 2, xin0, x0)
+    for dz in range(1, 8):
+        zo = (z + dz) % 8
+        last.append(rdma(xin0.at[me_x, :, zo], fin0.at[z], dev(xl, y, core, zo, xh)))
+    fin0[z] = xin0[me_x, :, z]
+    z_step(1, late_flows)
+    z_step(2, early_flows)
 
     for c in gather:
         c.wait_recv()
@@ -334,100 +457,14 @@
         nsend[k] = others[k * 8 : (k + 1) * 8]
     oth[0] = nsend[0]
 
-    for p in range(2, 4):
-        for d in y1[p]:
-            d.wait_recv()
-    weigh(rbw, rb, 1 - xl, 2 * Q)
-
-    def cols(ref, x, first, n):
-        return ref[first : first + n, pl.ds(side(x), 256)]
-
-    for x in range(2):
-        put(4 + x, tdot(cols(ow, x, 0, A), cols(ra, wrap(x, y == 3), 0, A)))
-        put(6 + x, tdot(cols(ra, x, 0, A), cols(ow, wrap(1 - x, y == 3), 0, A)))
-    pair1 = pair_sum(4, 4)
-    for x in range(2):
-        put(
-            8 + x,
-            tdot(cols(ow, x, 0, Q), cols(rb, wrap(1 - x, y == 0), 0, Q))
-            + tdot(cols(ow, x, 3 * Q + H1, H2), cols(rb, wrap(1 - x, y == 0), 2 * Q, H2)),
-        )
-        put(
-            10 + x,
-            tdot(cols(rb, x, 0, Q), cols(ow, wrap(x, y == 0), 0, Q))
-            + tdot(cols(rb, x, 2 * Q, H2), cols(ow, wrap(x, y == 0), 3 * Q + H1, H2)),
-        )
-    pair2 = pair_sum(8, 4)
-
-    flows = []
-    for g in range(3):
-        for way in (1, -1):
-            steps = 3 if (g % 2 == 0) == (way == 1) else 4
-            flows.append(dict(lo=4 + g * 2, way=way, steps=steps, target=up if way > 0 else down))
-
-    def z_step(s, which=(0, 6)):
-        for f, flow in list(enumerate(flows))[which[0] : which[1]]:
-            if s > flow["steps"]:
-                continue
-            if s:
-                flow["copy"].wait_recv()
-            if s == flow["steps"]:
-                continue
-            tiles = pl.ds(flow["lo"], 2)
-            here = (z + flow["way"] * (flow["steps"] - s) + 16) % 8
-            if s == 0:
-                src = inc.at[tiles, here]
-            else:
-                src = zl.at[f, s - 1]
-                src[...] = src[...] + inc[tiles, here]
-            flow["copy"] = rdma(src, zl.at[f, s], flow["target"])
-
-    pair_add(pair1, 4, 4)
-    z_step(0, (0, 4))
-    for x in range(2):
-        put(12 + x * 2, tdot(cols(rbw, x, 0, 2 * Q), cols(ra, wrap(x, ym >= 2), 0, 2 * Q)))
-        put(13 + x * 2, tdot(cols(ra, x, 0, 2 * Q), cols(rbw, wrap(x, yp >= 2), 0, 2 * Q)))
-    pair3 = pair_sum(12, 4)
-    pair_add(pair2, 8, 4)
-    z_step(0, (4, 6))
-    x1 = x_send(10, 1, xin1)
-    x_sum(0, 2, xin0, x0)
-    last = []
-    for dz in range(1, 8):
-        zo = (z + dz) % 8
-        last.append(rdma(xin0.at[me_x, :, zo], fin0.at[z], dev(xl, y, core, zo, xh)))
-    fin0[z] = xin0[me_x, :, z]
-    pair_add(pair3, 12, 4)
-    x2 = x_send(12, 2, xin2)
-    z_step(1)
     for k in range(1, 9):
         last.append(rdma(nsend.at[k], oth.at[k], {"pa": (pa + 16 - k) % 16, "af": af}))
-    x_sum(10, 1, xin1, x1)
-    for dz in range(8):
-        zo = (z + dz) % 8
-        last.append(rdma(xin1.at[me_x, 0, zo], fin1.at[z], dev(xl, ym, core, zo, xh)))
-    z_step(2)
+    z_step(2, late_flows)
     x_sum(12, 2, xin2, x2)
     for dz in range(8):
         zo = (z + dz) % 8
         last.append(rdma(xin2.at[me_x, 0, zo], fin2.at[z, 0], dev(xl, ym, core, zo, xh)))
         last.append(rdma(xin2.at[me_x, 1, zo], fin2.at[z, 1], dev(xl, yp, core, zo, xh)))
-    z_step(3)
-    z_step(4)
-    for g in range(3):
-        lo = 4 + g * 2
-        rz[lo - 4 : lo - 2] = (
-            inc[lo : lo + 2, z] + zl[2 * g, flows[2 * g]["steps"] - 1] + zl[2 * g + 1, flows[2 * g + 1]["steps"] - 1]
-        )
-    for dx in range(4):
-        xo, ho = xl ^ (dx % 2), xh ^ (dx // 2)
-        for slot in range(3):
-            if slot == 1:
-                last.append(rdma(rz.at[2 + xo, ho], fin3.at[me_x, 1], dev(xo, yp, core, z, ho)))
-            elif dx:
-                last.append(rdma(rz.at[2 * slot + xo, ho], fin3.at[me_x, slot], dev(xo, y, core, z, ho)))
-            else:
-                fin3[me_x, slot] = rz[2 * slot + xo, ho]
     for c in last:
         c.wait_recv()
 
@@ -435,9 +472,15 @@
         return functools.reduce(lambda p, q: p + q, parts)
 
     cross[:, 0:256] = total([fin0[s, 0] for s in range(8)])
-    cross[:, 256:512] = total([fin1[s] for s in range(8)] + [fin3[s, 0] for s in range(4)])
+    def kind_sum(kinds_of):
+        return total(
+            [fin3[s, t] for t in kinds_of for s in range(4)]
+            + [fin1[w, s, t] for t in kinds_of for w in range(2) for s in range(4)]
+        )
+
+    cross[:, 256:512] = kind_sum((0, 3))
     cross[:, 512:768] = total([fin2[s, t] for t in range(2) for s in range(8)])
-    cross[:, 768:1024] = total([fin3[s, t] for t in (1, 2) for s in range(4)])
+    cross[:, 768:1024] = kind_sum((1, 2))
     cross[:, 1024:1280] = total([fin0[s, 1] for s in range(8)])
     shift = pl.multiple_of(core * 128, 128)
     for k in range(9):
@@ -456,6 +499,7 @@
 def shards(spectra, tilt_min, tilt_max, tilt_axis):
     vmem = pl.BlockSpec(memory_space=pltpu.VMEM)
     scratch = [
+        pltpu.VMEM((3, 16, 128), jnp.int32),
         pltpu.VMEM((2, 2 * KC, 128), BF16),
         pltpu.VMEM((2, 2, KC, 128), BF16),
         pltpu.VMEM((KC, 128), BF16),
@@ -467,14 +511,13 @@
         pltpu.VMEM((16, 2, 8, 2, 8, 256), F32),
         pltpu.VMEM((16, 8, 2, 8, 256), F32),
         pltpu.VMEM((4, 2, 8, 8, 256), F32),
-        pltpu.VMEM((4, 1, 8, 8, 256), F32),
         pltpu.VMEM((4, 2, 8, 8, 256), F32),
-        pltpu.VMEM((6, 4, 2, 2, 8, 256), F32),
-        pltpu.VMEM((6, 2, 8, 256), F32),
+        pltpu.VMEM((8, 3, 2, 2, 8, 256), F32),
         pltpu.VMEM((8, 2, 8, 256), F32),
-        pltpu.VMEM((8, 8, 256), F32),
         pltpu.VMEM((8, 2, 8, 256), F32),
-        pltpu.VMEM((4, 3, 8, 256), F32),
+        pltpu.VMEM((2, 4, 4, 8, 256), F32),
+        pltpu.VMEM((8, 2, 8, 256), F32),
+        pltpu.VMEM((4, 4, 8, 256), F32),
         pltpu.VMEM((2, KC, 128), BF16),
         pltpu.VMEM((2, KC, 128), BF16),
         pltpu.VMEM((128, 128), F32),
@@ -487,7 +530,7 @@
         pltpu.VMEM((9, 8, 128), F32),
         pltpu.VMEM((9, 8, 128), F32),
         pltpu.VMEM((8, 1280), F32),
-        pltpu.SemaphoreType.DMA((6,)),
+        pltpu.SemaphoreType.DMA((9,)),
         pltpu.SemaphoreType.DMA((N_SEM,)),
         pltpu.SemaphoreType.DMA((N_SEM,)),
     ]
@@ -495,7 +538,7 @@
     return pl.pallas_call(
         kernel,
         out_shape=jax.ShapeDtypeStruct((8, 1152), F32),
-        in_specs=[pl.BlockSpec(memory_space=pl.ANY), vmem, vmem, vmem],
+        in_specs=[pl.BlockSpec(memory_space=pl.ANY)] * 4,
         out_specs=vmem,
         scratch_shapes=scratch,
         compiler_params=pltpu.CompilerParams(

time: 67.7 us -> 64.3 us (0.950)
  Pallas kernels: 66.1 us -> 62.4 us
    pallas_call x1, Pallas kernels: 66.1 us -> 62.4 us  [shards(): pl.pallas_call(kernel, out_shape=jax.ShapeDtypeStruct((8, 1152), F32), in...]
where the time goes in v4:
time: 64.3 us; the launch traced here: 63.8 us
  Pallas kernels  62.4 us (97%)
  local copies, waits for them, and re-layouts  1.39 us (2%)
    pallas_call x1, Pallas kernels, shards(): pl.pallas_call(kernel, out_shape=jax.ShapeDtypeStruct((8, 1152), F32), in...  62.4 us
    unnamed x1, local copies, waits for them, and re-layouts  1.39 us

profile of v4, /device:TPU:4, one launch (start us, length us, event | category | flops | bytes accessed | tf_op | source)
XLA Modules:
  0.0 63.8 jit_solution(12809614741843548641)
XLA Ops:
  0.0 62.4 %shard_map.46 = f32[8,1152]{1,0:T(8,128)} custom-call(bf16[2,3600,128]{2,1,0:T(8,128)(2,1)} %spec_hbm.1, s32[16,128]{1,0:T(8,128)} %bitcast.3, s32[16,128]{1,0:T(8,128)} %bitcast.4, s32[16,128]{1,0:T(8,128)} %bitcast.5), custom_call_target="tpu_custom_call" | custom-call | tf_op jit(solution)/shard_map/pallas_call | solution.py:538
  62.4 1.4 %copy.6 = f32[8,1152]{1,0:T(8,128)} copy(f32[8,1152]{1,0:T(8,128)} %shard_map.46) | data formatting | bytes 73728

commit v5 on v4

--- a/solution.py
+++ b/solution.py
@@ -50,11 +50,12 @@
     fy = jnp.where(iy < G // 2, iy, iy - G)
     return fx, fy, iz
 
-N_SEM = 256
+N_RECV = 65
+N_SEND = 40
 
 
 def kernel(spec_hbm, tmin_hbm, tmax_hbm, axis_hbm, out_ref, tilt, raw, m, wt, o, ow, ra, rb, rbw, acc, inc, xin0, xin2,
-           zl, rz, fin0, fin1, fin2, fin3, pw, cm, tt, tl, tg, tf, cls, hot, own, nsend, oth, cross, load_sem, ssem, rsem):
+           zl, rz, fin0, fin1, fin2, fin3, pw, cm, tt, tl, tg, tf, cls, hot, own, nsend, oth, cross, load_sem, ssem, rsem, gsend, grecv):
     xl, y, core, z, xh = coords()
     pa = lax.axis_index("pa")
     af = lax.axis_index("af")
@@ -65,12 +66,29 @@
 
     def rdma(src, dst, target):
         i = len(started)
+        if i >= N_SEND:
+            started[i - N_SEND].wait_send()
         c = pltpu.make_async_remote_copy(
-            src_ref=src, dst_ref=dst, send_sem=ssem.at[i], recv_sem=rsem.at[i], device_id=target, device_id_type=MESH
+            src_ref=src,
+            dst_ref=dst,
+            send_sem=ssem.at[i % N_SEND],
+            recv_sem=rsem.at[i],
+            device_id=target,
+            device_id_type=MESH,
         )
         c.start()
         started.append(c)
         return c
+
+    def in_group(g, src, dst, target):
+        return pltpu.make_async_remote_copy(
+            src_ref=src, dst_ref=dst, send_sem=gsend.at[g], recv_sem=grecv.at[g], device_id=target, device_id_type=MESH
+        )
+
+    def group_wait(g, size):
+        c = in_group(g, size, size, dev(xl, y, 1 - core, z, xh))
+        c.wait_recv()
+        c.wait_send()
 
     loads = []
     for i, ref in enumerate((tmin_hbm, tmax_hbm, axis_hbm)):
@@ -250,13 +268,13 @@
     to_minus(3, 2 * Q, Q)
     t_step(4)
     mine16 = rows16(z)
-    tg[xh, mine16, :] = tt[mine16, :] + tl[0, 2] + tl[1, 3]
-    gather = []
+    mine_g = pl.ds(pl.multiple_of(xh * 128 + z * 16, 16), 16)
+    tg[mine_g, :] = tt[mine16, :] + tl[0, 2] + tl[1, 3]
     for dz in range(8):
         for dh in range(2):
             if dz or dh:
-                part = tg.at[xh, mine16]
-                gather.append(rdma(part, part, dev(xl, y, core, (z + dz) % 8, xh ^ dh)))
+                part = tg.at[mine_g]
+                in_group(0, part, part, dev(xl, y, core, (z + dz) % 8, xh ^ dh)).start()
 
     x_other[2].wait_recv()
     to_plus(3, 0, Q, Q)
@@ -335,7 +353,6 @@
     x0 = x_send(0, 2, xin0)
 
     owners = (y, yp, y, ym)
-    last = []
     flows = []
     for g in range(4):
         for way in (1, -1):
@@ -375,13 +392,12 @@
                 for i in range(2):
                     kind, late = (flow["lo"] + i) % 4, f // 4
                     for ho in (xh, 1 - xh):
-                        last.append(
-                            rdma(
-                                zl.at[f, 2, i, ho],
-                                fin1.at[(1 - way) // 2, me_x, kind],
-                                dev(early[kind] ^ late, owners[kind], core, rows_for(1), ho),
-                            )
-                        )
+                        in_group(
+                            1,
+                            zl.at[f, 2, i, ho],
+                            fin1.at[(1 - way) // 2, me_x, kind],
+                            dev(early[kind] ^ late, owners[kind], core, rows_for(1), ho),
+                        ).start()
 
     def own_rows():
         for kind in range(4):
@@ -391,9 +407,9 @@
             xo, ho = xl ^ (dx % 2), xh ^ (dx // 2)
             for kind, yo in enumerate(owners):
                 if dx or kind % 2:
-                    last.append(rdma(rz.at[2 * kind + xo, ho], fin3.at[me_x, kind], dev(xo, yo, core, z, ho)))
+                    in_group(2, rz.at[2 * kind + xo, ho], fin3.at[me_x * 4 + kind], dev(xo, yo, core, z, ho)).start()
                 else:
-                    fin3[me_x, kind] = rz[2 * kind + xo, ho]
+                    fin3[me_x * 4 + kind] = rz[2 * kind + xo, ho]
 
     pair_add(pair1, 4, 4)
     z_step(0, early_flows)
@@ -415,14 +431,13 @@
     x_sum(0, 2, xin0, x0)
     for dz in range(1, 8):
         zo = (z + dz) % 8
-        last.append(rdma(xin0.at[me_x, :, zo], fin0.at[z], dev(xl, y, core, zo, xh)))
+        in_group(3, xin0.at[me_x, :, zo], fin0.at[z], dev(xl, y, core, zo, xh)).start()
     fin0[z] = xin0[me_x, :, z]
     z_step(1, late_flows)
     z_step(2, early_flows)
 
-    for c in gather:
-        c.wait_recv()
-    tf[...] = tg[0] + tg[1]
+    group_wait(0, tg.at[0:240])
+    tf[...] = tg[0:128] + tg[128:256]
 
     def split(value):
         hi = value.astype(BF16).astype(F32)
@@ -458,15 +473,20 @@
     oth[0] = nsend[0]
 
     for k in range(1, 9):
-        last.append(rdma(nsend.at[k], oth.at[k], {"pa": (pa + 16 - k) % 16, "af": af}))
+        in_group(4, nsend.at[k], oth.at[k], {"pa": (pa + 16 - k) % 16, "af": af}).start()
     z_step(2, late_flows)
     x_sum(12, 2, xin2, x2)
     for dz in range(8):
         zo = (z + dz) % 8
-        last.append(rdma(xin2.at[me_x, 0, zo], fin2.at[z, 0], dev(xl, ym, core, zo, xh)))
-        last.append(rdma(xin2.at[me_x, 1, zo], fin2.at[z, 1], dev(xl, yp, core, zo, xh)))
-    for c in last:
-        c.wait_recv()
+        in_group(5, xin2.at[me_x, 0, zo], fin2.at[z, 0], dev(xl, ym, core, zo, xh)).start()
+        in_group(5, xin2.at[me_x, 1, zo], fin2.at[z, 1], dev(xl, yp, core, zo, xh)).start()
+    for c in started[-N_SEND:]:
+        c.wait_send()
+    group_wait(3, fin0.at[0:7])
+    group_wait(4, oth.at[0:8])
+    group_wait(2, fin3.at[0:14])
+    group_wait(1, fin1)
+    group_wait(5, fin2)
 
     def total(parts):
         return functools.reduce(lambda p, q: p + q, parts)
@@ -474,7 +494,7 @@
     cross[:, 0:256] = total([fin0[s, 0] for s in range(8)])
     def kind_sum(kinds_of):
         return total(
-            [fin3[s, t] for t in kinds_of for s in range(4)]
+            [fin3[s * 4 + t] for t in kinds_of for s in range(4)]
             + [fin1[w, s, t] for t in kinds_of for w in range(2) for s in range(4)]
         )
 
@@ -488,8 +508,6 @@
         out_ref[:, here] = cross[:, pl.ds(pl.multiple_of(shift + k * 128, 128), 128)] / jnp.sqrt(
             own[:, here] * oth[k] + eps_norm
         )
-    for c in started:
-        c.wait_send()
 
 
 def slopes(degrees):
@@ -517,12 +535,12 @@
         pltpu.VMEM((8, 2, 8, 256), F32),
         pltpu.VMEM((2, 4, 4, 8, 256), F32),
         pltpu.VMEM((8, 2, 8, 256), F32),
-        pltpu.VMEM((4, 4, 8, 256), F32),
+        pltpu.VMEM((16, 8, 256), F32),
         pltpu.VMEM((2, KC, 128), BF16),
         pltpu.VMEM((2, KC, 128), BF16),
         pltpu.VMEM((128, 128), F32),
         pltpu.VMEM((2, 4, 16, 128), F32),
-        pltpu.VMEM((2, 128, 128), F32),
+        pltpu.VMEM((256, 128), F32),
         pltpu.VMEM((128, 128), F32),
         pltpu.VMEM((2, 16, 128), jnp.int32),
         pltpu.VMEM((128, 1152), BF16),
@@ -531,8 +549,10 @@
         pltpu.VMEM((9, 8, 128), F32),
         pltpu.VMEM((8, 1280), F32),
         pltpu.SemaphoreType.DMA((9,)),
-        pltpu.SemaphoreType.DMA((N_SEM,)),
-        pltpu.SemaphoreType.DMA((N_SEM,)),
+        pltpu.SemaphoreType.DMA((N_SEND,)),
+        pltpu.SemaphoreType.DMA((N_RECV,)),
+        pltpu.SemaphoreType.DMA((6,)),
+        pltpu.SemaphoreType.DMA((6,)),
     ]
     tilts = [t.reshape(16, 128) for t in (tilt_min, tilt_max, tilt_axis)]
     return pl.pallas_call(

time: 64.3 us -> 60.5 us (0.941)
  Pallas kernels: 62.4 us -> 58.6 us
    pallas_call x1, Pallas kernels: 62.4 us -> 58.6 us  [shards(): pl.pallas_call(kernel, out_shape=jax.ShapeDtypeStruct((8, 1152), F32), in...]
where the time goes in v5:
time: 60.5 us; the launch traced here: 60 us
  Pallas kernels  58.6 us (97%)
  local copies, waits for them, and re-layouts  1.39 us (2%)
    pallas_call x1, Pallas kernels, shards(): pl.pallas_call(kernel, out_shape=jax.ShapeDtypeStruct((8, 1152), F32), in...  58.6 us
    unnamed x1, local copies, waits for them, and re-layouts  1.39 us

profile of v5, /device:TPU:4, one launch (start us, length us, event | category | flops | bytes accessed | tf_op | source)
XLA Modules:
  0.0 60.0 jit_solution(6400373154848987622)
XLA Ops:
  0.0 58.6 %shard_map.46 = f32[8,1152]{1,0:T(8,128)} custom-call(bf16[2,3600,128]{2,1,0:T(8,128)(2,1)} %spec_hbm.1, s32[16,128]{1,0:T(8,128)} %bitcast.3, s32[16,128]{1,0:T(8,128)} %bitcast.4, s32[16,128]{1,0:T(8,128)} %bitcast.5), custom_call_target="tpu_custom_call" | custom-call | tf_op jit(solution)/shard_map/pallas_call | solution.py:558
  58.6 1.4 %copy.6 = f32[8,1152]{1,0:T(8,128)} copy(f32[8,1152]{1,0:T(8,128)} %shard_map.46) | data formatting | bytes 73728

commit v6 on v5

--- a/solution.py
+++ b/solution.py
@@ -50,8 +50,8 @@
     fy = jnp.where(iy < G // 2, iy, iy - G)
     return fx, fy, iz
 
-N_RECV = 65
-N_SEND = 40
+N_RECV = 70
+N_SEND = 32
 
 
 def kernel(spec_hbm, tmin_hbm, tmax_hbm, axis_hbm, out_ref, tilt, raw, m, wt, o, ow, ra, rb, rbw, acc, inc, xin0, xin2,
@@ -247,15 +247,16 @@
 
     by_chunk(core, weights)
 
-    def weigh(dst, src, x, n):
+    def weigh(dst, src, x, first, n):
+        rows = slice(first, first + n)
         for dc in range(2):
             here = pl.ds(pl.multiple_of(x * 256 + dc * 128, 128), 128)
-            dst[:, here] = src[0:n, here] * wt[0:n, :]
+            dst[rows, here] = src[rows, here] * wt[rows, :]
 
     x_same[0].wait_recv()
     y_high(2)
     t_step(1)
-    weigh(ow, o, xl, KC)
+    weigh(ow, o, xl, 0, KC)
     x_same[1].wait_recv()
     y_low(2)
     t_step(2)
@@ -276,12 +277,6 @@
                 part = tg.at[mine_g]
                 in_group(0, part, part, dev(xl, y, core, (z + dz) % 8, xh ^ dh)).start()
 
-    x_other[2].wait_recv()
-    to_plus(3, 0, Q, Q)
-    x_other[3].wait_recv()
-    to_minus(3, Q, Q)
-    weigh(ow, o, 1 - xl, KC)
-
     def put(tile, value):
         acc[tile] = value.reshape(2, 8, 2, 8, 256)
 
@@ -300,9 +295,27 @@
         for t in range(lo, lo + n):
             inc[t] = inc[t] + acc[t, core]
 
-    for x in range(2):
-        for slot, xo in ((0, x), (1, 1 - x)):
-            put(x * 2 + slot, tdot(ow[:, x * 256 : x * 256 + 256], o[:, xo * 256 : xo * 256 + 256]))
+    def cols(ref, x, first, n):
+        return ref[first : first + n, pl.ds(side(x), 256)]
+
+    def add(tile, value):
+        acc[tile] = acc[tile] + value.reshape(2, 8, 2, 8, 256)
+
+    def own_tiles(first, n, store):
+        for x in range(2):
+            for slot, xo in ((0, x), (1, 1 - x)):
+                store(x * 2 + slot, tdot(cols(ow, x, first, n), cols(o, xo, first, n)))
+
+    weigh(ow, o, 1 - xl, 2 * Q, 2 * Q)
+    own_tiles(2 * Q, 2 * Q, put)
+    x_other[2].wait_recv()
+    to_plus(3, 0, Q, Q)
+    weigh(ow, o, 1 - xl, 0, Q)
+    own_tiles(0, Q, add)
+    x_other[3].wait_recv()
+    to_minus(3, Q, Q)
+    weigh(ow, o, 1 - xl, Q, Q)
+    own_tiles(Q, Q, add)
     pair0 = pair_sum(0, 4)
 
     def x_send(lo, n, buf):
@@ -322,16 +335,16 @@
             total = total + buf[(xh ^ (dx // 2)) * 2 + (xl ^ (dx % 2))]
         buf[me_x] = total
 
-    def cols(ref, x, first, n):
-        return ref[first : first + n, pl.ds(side(x), 256)]
-
     early = (wrap(xl, y == 3), xl, wrap(1 - xl, y == 0), xl)
 
-    def kinds(lo, late):
-        x0, x1, x2, x3 = (x ^ late for x in early)
+    def plus_kinds(lo, late, first, n, store):
+        x0, x1 = early[0] ^ late, early[1] ^ late
+        store(lo, tdot(cols(ow, x0, first, n), cols(ra, xl ^ late, first, n)))
+        store(lo + 1, tdot(cols(ra, x1, first, n), cols(ow, wrap(1 - x1, y == 3), first, n)))
+
+    def minus_kinds(lo, late):
+        x2, x3 = early[2] ^ late, early[3] ^ late
         xr = xl ^ late
-        put(lo, tdot(cols(ow, x0, 0, A), cols(ra, xr, 0, A)))
-        put(lo + 1, tdot(cols(ra, x1, 0, A), cols(ow, wrap(1 - x1, y == 3), 0, A)))
         put(
             lo + 2,
             tdot(cols(ow, x2, 0, Q), cols(rb, xr, 0, Q))
@@ -342,13 +355,22 @@
             tdot(cols(rb, x3, 0, Q), cols(ow, wrap(x3, y == 0), 0, Q))
             + tdot(cols(rb, x3, 2 * Q, H2), cols(ow, wrap(x3, y == 0), 3 * Q + H1, H2)),
         )
-        return pair_sum(lo, 4)
+
+    def second_minus(first, n, store):
+        for x in range(2):
+            store(12 + x, tdot(cols(rbw, x, first, n), cols(ra, wrap(x, ym >= 2), first, n)))
+
+    def second_plus(first, n, store):
+        for x in range(2):
+            store(14 + x, tdot(cols(ra, x, first, n), cols(rbw, wrap(x, yp >= 2), first, n)))
 
     for p in range(2):
         for d in y1[p]:
             d.wait_recv()
-    pair1 = kinds(4, 0)
-    weigh(rbw, rb, xl, 2 * Q)
+    plus_kinds(4, 0, 0, A, put)
+    minus_kinds(4, 0)
+    pair1 = pair_sum(4, 4)
+    weigh(rbw, rb, xl, 0, 2 * Q)
     pair_add(pair0, 0, 4)
     x0 = x_send(0, 2, xin0)
 
@@ -413,29 +435,30 @@
 
     pair_add(pair1, 4, 4)
     z_step(0, early_flows)
-    for p in range(2, 4):
-        for d in y1[p]:
-            d.wait_recv()
-    weigh(rbw, rb, 1 - xl, 2 * Q)
-    for x in range(2):
-        put(12 + x * 2, tdot(cols(rbw, x, 0, 2 * Q), cols(ra, wrap(x, ym >= 2), 0, 2 * Q)))
-        put(13 + x * 2, tdot(cols(ra, x, 0, 2 * Q), cols(rbw, wrap(x, yp >= 2), 0, 2 * Q)))
-    pair3 = pair_sum(12, 4)
-    pair2 = kinds(8, 1)
-    pair_add(pair3, 12, 4)
-    x2 = x_send(12, 2, xin2)
-    pair_add(pair2, 8, 4)
-    z_step(0, late_flows)
+    for d in y1[2] + y1[3][:-1]:
+        d.wait_recv()
+    minus_kinds(8, 1)
+    pair_b = pair_sum(10, 2)
+    weigh(rbw, rb, 1 - xl, 0, 2 * Q)
+    second_minus(Q, Q, put)
+    second_plus(Q, Q, put)
+    plus_kinds(8, 1, Q, Q + H1, put)
+    pair_add(pair_b, 10, 2)
+    z_step(0, (6, 8))
+    y1[3][-1].wait_recv()
+    second_minus(0, Q, add)
+    pair_c = pair_sum(12, 2)
+    second_plus(0, Q, add)
+    pair_d = pair_sum(14, 2)
+    plus_kinds(8, 1, 0, Q, add)
+    pair_a = pair_sum(8, 2)
+    pair_add(pair_c, 12, 2)
+    x2 = x_send(12, 1, xin2.at[0])
+    pair_add(pair_d, 14, 2)
+    x3 = x_send(14, 1, xin2.at[1])
+    pair_add(pair_a, 8, 2)
+    z_step(0, (4, 6))
     z_step(1, early_flows)
-    own_rows()
-    x_sum(0, 2, xin0, x0)
-    for dz in range(1, 8):
-        zo = (z + dz) % 8
-        in_group(3, xin0.at[me_x, :, zo], fin0.at[z], dev(xl, y, core, zo, xh)).start()
-    fin0[z] = xin0[me_x, :, z]
-    z_step(1, late_flows)
-    z_step(2, early_flows)
-
     group_wait(0, tg.at[0:240])
     tf[...] = tg[0:128] + tg[128:256]
 
@@ -474,12 +497,23 @@
 
     for k in range(1, 9):
         in_group(4, nsend.at[k], oth.at[k], {"pa": (pa + 16 - k) % 16, "af": af}).start()
-    z_step(2, late_flows)
-    x_sum(12, 2, xin2, x2)
-    for dz in range(8):
+    z_step(1, (6, 8))
+    x_sum(0, 2, xin0, x0)
+    for dz in range(1, 8):
         zo = (z + dz) % 8
-        in_group(5, xin2.at[me_x, 0, zo], fin2.at[z, 0], dev(xl, ym, core, zo, xh)).start()
-        in_group(5, xin2.at[me_x, 1, zo], fin2.at[z, 1], dev(xl, yp, core, zo, xh)).start()
+        in_group(3, xin0.at[me_x, :, zo], fin0.at[z], dev(xl, y, core, zo, xh)).start()
+    fin0[z] = xin0[me_x, :, z]
+    z_step(1, (4, 6))
+    z_step(2, early_flows)
+    z_step(2, (6, 8))
+    own_rows()
+
+    z_step(2, (4, 6))
+    for i, (copies, yo) in enumerate(((x2, ym), (x3, yp))):
+        x_sum(12 + 2 * i, 1, xin2.at[i], copies)
+        for dz in (4, 3, 5, 2, 6, 1, 7, 0):
+            zo = (z + dz) % 8
+            in_group(5, xin2.at[i, me_x, 0, zo], fin2.at[z, i], dev(xl, yo, core, zo, xh)).start()
     for c in started[-N_SEND:]:
         c.wait_send()
     group_wait(3, fin0.at[0:7])
@@ -529,7 +563,7 @@
         pltpu.VMEM((16, 2, 8, 2, 8, 256), F32),
         pltpu.VMEM((16, 8, 2, 8, 256), F32),
         pltpu.VMEM((4, 2, 8, 8, 256), F32),
-        pltpu.VMEM((4, 2, 8, 8, 256), F32),
+        pltpu.VMEM((2, 4, 1, 8, 8, 256), F32),
         pltpu.VMEM((8, 3, 2, 2, 8, 256), F32),
         pltpu.VMEM((8, 2, 8, 256), F32),
         pltpu.VMEM((8, 2, 8, 256), F32),

time: 60.5 us -> 58.9 us (0.974)
  Pallas kernels: 58.6 us -> 56.6 us
    pallas_call x1, Pallas kernels: 58.6 us -> 56.6 us  [shards(): pl.pallas_call(kernel, out_shape=jax.ShapeDtypeStruct((8, 1152), F32), in...]
where the time goes in v6:
time: 58.9 us; the launch traced here: 58 us
  Pallas kernels  56.6 us (96%)
  local copies, waits for them, and re-layouts  1.39 us (2%)
    pallas_call x1, Pallas kernels, shards(): pl.pallas_call(kernel, out_shape=jax.ShapeDtypeStruct((8, 1152), F32), in...  56.6 us
    unnamed x1, local copies, waits for them, and re-layouts  1.39 us

profile of v6, /device:TPU:4, one launch (start us, length us, event | category | flops | bytes accessed | tf_op | source)
XLA Modules:
  0.0 58.0 jit_solution(4339605800707216587)
XLA Ops:
  0.0 56.6 %shard_map.46 = f32[8,1152]{1,0:T(8,128)} custom-call(bf16[2,3600,128]{2,1,0:T(8,128)(2,1)} %spec_hbm.1, s32[16,128]{1,0:T(8,128)} %bitcast.3, s32[16,128]{1,0:T(8,128)} %bitcast.4, s32[16,128]{1,0:T(8,128)} %bitcast.5), custom_call_target="tpu_custom_call" | custom-call | tf_op jit(solution)/shard_map/pallas_call | solution.py:592
  56.6 1.4 %copy.6 = f32[8,1152]{1,0:T(8,128)} copy(f32[8,1152]{1,0:T(8,128)} %shard_map.46) | data formatting | bytes 73728

commit v7 on v6

--- a/solution.py
+++ b/solution.py
@@ -50,7 +50,7 @@
     fy = jnp.where(iy < G // 2, iy, iy - G)
     return fx, fy, iz
 
-N_RECV = 70
+N_RECV = 72
 N_SEND = 32
 
 
@@ -90,18 +90,6 @@
         c.wait_recv()
         c.wait_send()
 
-    loads = []
-    for i, ref in enumerate((tmin_hbm, tmax_hbm, axis_hbm)):
-        c = pltpu.make_async_copy(ref, tilt.at[i], load_sem.at[i])
-        c.start()
-        loads.append(c)
-    tmin_ref, tmax_ref, axis_ref = tilt.at[0], tilt.at[1], tilt.at[2]
-    for first, n in ((core * KC, MID), (MID, KC - MID), ((1 - core) * KC, MID)):
-        here = pl.ds(first if isinstance(first, int) else pl.multiple_of(first, 16), n)
-        for p in range(2):
-            c = pltpu.make_async_copy(spec_hbm.at[p, here], raw.at[p, here], load_sem.at[len(loads)])
-            c.start()
-            loads.append(c)
     barrier = pltpu.get_barrier_semaphore()
     peers = [
         dev(xl, y, 1 - core, z, xh),
@@ -115,6 +103,18 @@
     ]
     for peer in peers:
         pl.semaphore_signal(barrier, inc=1, device_id=peer, device_id_type=MESH)
+    loads = []
+    for i, ref in enumerate((tmin_hbm, tmax_hbm, axis_hbm)):
+        c = pltpu.make_async_copy(ref, tilt.at[i], load_sem.at[i])
+        c.start()
+        loads.append(c)
+    tmin_ref, tmax_ref, axis_ref = tilt.at[0], tilt.at[1], tilt.at[2]
+    for first, n in ((core * KC, MID), (MID, KC - MID), ((1 - core) * KC, MID)):
+        here = pl.ds(first if isinstance(first, int) else pl.multiple_of(first, 16), n)
+        for p in range(2):
+            c = pltpu.make_async_copy(spec_hbm.at[p, here], raw.at[p, here], load_sem.at[len(loads)])
+            c.start()
+            loads.append(c)
     raw[:, VD:, :] = jnp.zeros((2, 2 * KC - VD, 128), BF16)
 
     for c in loads[:3]:
@@ -156,7 +156,7 @@
 
     for c in loads[3:7]:
         c.wait()
-    mask_half(core, (2, 4))
+    mask_half(core, (3, 4))
     pl.semaphore_wait(barrier, len(peers))
 
     col = own_col(0, 0)
@@ -183,13 +183,22 @@
     def to_x(half, r0, n, target):
         return rdma(m.at[1 - xl, half, pl.ds(r0, n)], o.at[pl.ds(r0, n), pl.ds(col, 128)], target)
 
-    own_high, own_low = pl.ds(2 * Q, 2 * Q), pl.ds(0, 2 * Q)
-    x_same = [to_x(core, 2 * Q, 2 * Q, dev(1 - xl, y, core, z, xh))]
-    o[own_high, pl.ds(col, 128)] = m[xl, core, own_high]
-    y_high(0)
-    mask_half(core, (0, 2))
-    x_same.append(to_x(core, 0, 2 * Q, dev(1 - xl, y, core, z, xh)))
-    o[own_low, pl.ds(col, 128)] = m[xl, core, own_low]
+    x_same = []
+
+    def first(slots, r0, n):
+        if slots:
+            mask_half(core, slots)
+        here = pl.ds(r0, n)
+        x_same.append(to_x(core, r0, n, dev(1 - xl, y, core, z, xh)))
+        o[here, pl.ds(col, 128)] = m[xl, core, here]
+
+    first(None, 3 * Q, Q)
+    to_plus(0, 3 * Q, Q, 0)
+    to_minus(0, 3 * Q, H1)
+    first((2, 3), 2 * Q, Q)
+    to_minus(0, 2 * Q, Q)
+    to_plus(0, 2 * Q + H1, H2, 2 * Q)
+    first((0, 2), 0, 2 * Q)
     y_low(0)
     for c in loads[7:]:
         c.wait()
@@ -254,10 +263,11 @@
             dst[rows, here] = src[rows, here] * wt[rows, :]
 
     x_same[0].wait_recv()
+    x_same[1].wait_recv()
     y_high(2)
     t_step(1)
     weigh(ow, o, xl, 0, KC)
-    x_same[1].wait_recv()
+    x_same[2].wait_recv()
     y_low(2)
     t_step(2)
     x_other[0].wait_recv()
@@ -591,7 +601,7 @@
     tilts = [t.reshape(16, 128) for t in (tilt_min, tilt_max, tilt_axis)]
     return pl.pallas_call(
         kernel,
-        out_shape=jax.ShapeDtypeStruct((8, 1152), F32),
+        out_shape=pltpu.VMEM((8, 1152), F32),
         in_specs=[pl.BlockSpec(memory_space=pl.ANY)] * 4,
         out_specs=vmem,
         scratch_shapes=scratch,

time: 58.9 us -> 57.4 us (0.975)
  Pallas kernels: 56.6 us -> 55.8 us
  local copies, waits for them, and re-layouts: 1.39 us -> 0.62 us
    pallas_call x1, Pallas kernels: 56.6 us -> 55.8 us  [shards(): pl.pallas_call(kernel, out_shape=pltpu.VMEM((8, 1152), F32), in_specs=[pl...]
    unnamed x1, local copies, waits for them, and re-layouts: 1.39 us -> 0.62 us
where the time goes in v7:
time: 57.4 us; the launch traced here: 56.4 us
  Pallas kernels  55.8 us (97%)
  local copies, waits for them, and re-layouts  0.62 us (1%)
    pallas_call x1, Pallas kernels, shards(): pl.pallas_call(kernel, out_shape=pltpu.VMEM((8, 1152), F32), in_specs=[pl...  55.8 us

profile of v7, /device:TPU:4, one launch (start us, length us, event | category | flops | bytes accessed | tf_op | source)
XLA Modules:
  0.0 56.4 jit_solution(11146785637018945882)
XLA Ops:
  0.0 55.8 %shard_map.46 = f32[8,1152]{1,0:T(8,128)S(1)} custom-call(bf16[2,3600,128]{2,1,0:T(8,128)(2,1)} %spec_hbm.1, s32[16,128]{1,0:T(8,128)} %bitcast.3, s32[16,128]{1,0:T(8,128)} %bitcast.4, s32[16,128]{1,0:T(8,128)} %bitcast.5), custom_call_target="tpu_custom_call" | custom-call | tf_op jit(solution)/shard_map/pallas_call | solution.py:602
  55.8 0.6 %copy.6 = f32[8,1152]{1,0:T(8,128)} copy(f32[8,1152]{1,0:T(8,128)S(1)} %shard_map.46) | data formatting | bytes 73728

commit v8 on v7

--- a/solution.py
+++ b/solution.py
@@ -50,7 +50,7 @@
     fy = jnp.where(iy < G // 2, iy, iy - G)
     return fx, fy, iz
 
-N_RECV = 72
+N_RECV = 74
 N_SEND = 32
 
 
@@ -204,7 +204,10 @@
         c.wait()
     mask_half(1 - core)
     sib = rdma(m.at[xl, 1 - core], o.at[:, pl.ds(col, 128)], dev(xl, y, 1 - core, z, xh))
-    x_other = [to_x(1 - core, q * Q, Q, dev(1 - xl, y, 1 - core, z, xh)) for q in (3, 2, 0, 1)]
+    x_other = [
+        to_x(1 - core, r0, n, dev(1 - xl, y, 1 - core, z, xh))
+        for r0, n in ((3 * Q, Q), (2 * Q, Q), (0, Q), (Q, H1), (Q + H1, H2))
+    ]
 
     for half in range(2):
 
@@ -278,6 +281,48 @@
     to_plus(3, 2 * Q + H1, H2, 2 * Q)
     to_minus(3, 2 * Q, Q)
     t_step(4)
+    def put(tile, value):
+        acc[tile] = value.reshape(2, 8, 2, 8, 256)
+
+    def side(x):
+        return pl.multiple_of(x * 256, 256)
+
+    def wrap(x, cond):
+        return x ^ cond.astype(jnp.int32)
+
+    def pair_sum(lo, n):
+        tiles = pl.ds(lo, n)
+        return rdma(acc.at[tiles, 1 - core], inc.at[tiles], dev(xl, y, 1 - core, z, xh))
+
+    def pair_add(copy, lo, n):
+        copy.wait_recv()
+        for t in range(lo, lo + n):
+            inc[t] = inc[t] + acc[t, core]
+
+    def cols(ref, x, first, n):
+        return ref[first : first + n, pl.ds(side(x), 256)]
+
+    def add(tile, value):
+        acc[tile] = acc[tile] + value.reshape(2, 8, 2, 8, 256)
+
+    def own_tiles(first, n, store):
+        for x in range(2):
+            for slot, xo in ((0, x), (1, 1 - x)):
+                store(x * 2 + slot, tdot(cols(ow, x, first, n), cols(o, xo, first, n)))
+
+    weigh(ow, o, 1 - xl, 2 * Q, 2 * Q)
+    own_tiles(2 * Q, 2 * Q, put)
+    x_other[2].wait_recv()
+    to_plus(3, 0, Q, Q)
+    weigh(ow, o, 1 - xl, 0, Q)
+    own_tiles(0, Q, add)
+    x_other[3].wait_recv()
+    to_minus(3, Q, H1)
+    x_other[4].wait_recv()
+    to_minus(3, Q + H1, H2)
+    weigh(ow, o, 1 - xl, Q, Q)
+    own_tiles(Q, Q, add)
+    pair0 = pair_sum(0, 4)
     mine16 = rows16(z)
     mine_g = pl.ds(pl.multiple_of(xh * 128 + z * 16, 16), 16)
     tg[mine_g, :] = tt[mine16, :] + tl[0, 2] + tl[1, 3]
@@ -287,46 +332,6 @@
                 part = tg.at[mine_g]
                 in_group(0, part, part, dev(xl, y, core, (z + dz) % 8, xh ^ dh)).start()
 
-    def put(tile, value):
-        acc[tile] = value.reshape(2, 8, 2, 8, 256)
-
-    def side(x):
-        return pl.multiple_of(x * 256, 256)
-
-    def wrap(x, cond):
-        return x ^ cond.astype(jnp.int32)
-
-    def pair_sum(lo, n):
-        tiles = pl.ds(lo, n)
-        return rdma(acc.at[tiles, 1 - core], inc.at[tiles], dev(xl, y, 1 - core, z, xh))
-
-    def pair_add(copy, lo, n):
-        copy.wait_recv()
-        for t in range(lo, lo + n):
-            inc[t] = inc[t] + acc[t, core]
-
-    def cols(ref, x, first, n):
-        return ref[first : first + n, pl.ds(side(x), 256)]
-
-    def add(tile, value):
-        acc[tile] = acc[tile] + value.reshape(2, 8, 2, 8, 256)
-
-    def own_tiles(first, n, store):
-        for x in range(2):
-            for slot, xo in ((0, x), (1, 1 - x)):
-                store(x * 2 + slot, tdot(cols(ow, x, first, n), cols(o, xo, first, n)))
-
-    weigh(ow, o, 1 - xl, 2 * Q, 2 * Q)
-    own_tiles(2 * Q, 2 * Q, put)
-    x_other[2].wait_recv()
-    to_plus(3, 0, Q, Q)
-    weigh(ow, o, 1 - xl, 0, Q)
-    own_tiles(0, Q, add)
-    x_other[3].wait_recv()
-    to_minus(3, Q, Q)
-    weigh(ow, o, 1 - xl, Q, Q)
-    own_tiles(Q, Q, add)
-    pair0 = pair_sum(0, 4)
 
     def x_send(lo, n, buf):
         copies = []

time: 57.4 us -> 57.6 us (level)
  no operation moved by 1% of the time
where the time goes in v8:
time: 57.6 us; the launch traced here: 56.8 us
  Pallas kernels  56.2 us (98%)
  local copies, waits for them, and re-layouts  0.62 us (1%)
    pallas_call x1, Pallas kernels, shards(): pl.pallas_call(kernel, out_shape=pltpu.VMEM((8, 1152), F32), in_specs=[pl...  56.2 us

profile of v8, /device:TPU:4, one launch (start us, length us, event | category | flops | bytes accessed | tf_op | source)
XLA Modules:
  0.0 56.8 jit_solution(12522859745687370704)
XLA Ops:
  0.0 56.2 %shard_map.46 = f32[8,1152]{1,0:T(8,128)S(1)} custom-call(bf16[2,3600,128]{2,1,0:T(8,128)(2,1)} %spec_hbm.1, s32[16,128]{1,0:T(8,128)} %bitcast.3, s32[16,128]{1,0:T(8,128)} %bitcast.4, s32[16,128]{1,0:T(8,128)} %bitcast.5), custom_call_target="tpu_custom_call" | custom-call | tf_op jit(solution)/shard_map/pallas_call | solution.py:607
  56.2 0.6 %copy.6 = f32[8,1152]{1,0:T(8,128)} copy(f32[8,1152]{1,0:T(8,128)S(1)} %shard_map.46) | data formatting | bytes 73728

commit v9 on v7

--- a/solution.py
+++ b/solution.py
@@ -529,29 +529,32 @@
     group_wait(3, fin0.at[0:7])
     group_wait(4, oth.at[0:8])
     group_wait(2, fin3.at[0:14])
-    group_wait(1, fin1)
-    group_wait(5, fin2)
 
     def total(parts):
         return functools.reduce(lambda p, q: p + q, parts)
 
+    def near(kinds_of):
+        return total([fin3[s * 4 + t] for t in kinds_of for s in range(4)])
+
+    def passed_on(kinds_of):
+        return total([fin1[w, s, t] for t in kinds_of for w in range(2) for s in range(4)])
+
     cross[:, 0:256] = total([fin0[s, 0] for s in range(8)])
-    def kind_sum(kinds_of):
-        return total(
-            [fin3[s * 4 + t] for t in kinds_of for s in range(4)]
-            + [fin1[w, s, t] for t in kinds_of for w in range(2) for s in range(4)]
-        )
-
-    cross[:, 256:512] = kind_sum((0, 3))
+    cross[:, 1024:1280] = total([fin0[s, 1] for s in range(8)])
+    cross[:, 256:512] = near((0, 3))
+    cross[:, 768:1024] = near((1, 2))
+    for k in range(9):
+        here = slice(k * 128, (k + 1) * 128)
+        own[:, here] = jnp.sqrt(own[:, here] * oth[k] + eps_norm)
+    group_wait(1, fin1)
+    cross[:, 256:512] = cross[:, 256:512] + passed_on((0, 3))
+    cross[:, 768:1024] = cross[:, 768:1024] + passed_on((1, 2))
+    group_wait(5, fin2)
     cross[:, 512:768] = total([fin2[s, t] for t in range(2) for s in range(8)])
-    cross[:, 768:1024] = kind_sum((1, 2))
-    cross[:, 1024:1280] = total([fin0[s, 1] for s in range(8)])
     shift = pl.multiple_of(core * 128, 128)
     for k in range(9):
         here = slice(k * 128, (k + 1) * 128)
-        out_ref[:, here] = cross[:, pl.ds(pl.multiple_of(shift + k * 128, 128), 128)] / jnp.sqrt(
-            own[:, here] * oth[k] + eps_norm
-        )
+        out_ref[:, here] = cross[:, pl.ds(pl.multiple_of(shift + k * 128, 128), 128)] / own[:, here]
 
 
 def slopes(degrees):

time: 57.4 us -> 57.4 us (level)
  no operation moved by 1% of the time
where the time goes in v9:
time: 57.4 us; the launch traced here: 56.3 us
  Pallas kernels  55.7 us (97%)
  local copies, waits for them, and re-layouts  0.62 us (1%)
    pallas_call x1, Pallas kernels, shards(): pl.pallas_call(kernel, out_shape=pltpu.VMEM((8, 1152), F32), in_specs=[pl...  55.7 us

profile of v9, /device:TPU:4, one launch (start us, length us, event | category | flops | bytes accessed | tf_op | source)
XLA Modules:
  0.0 56.3 jit_solution(9138951610825624844)
XLA Ops:
  0.0 55.7 %shard_map.46 = f32[8,1152]{1,0:T(8,128)S(1)} custom-call(bf16[2,3600,128]{2,1,0:T(8,128)(2,1)} %spec_hbm.1, s32[16,128]{1,0:T(8,128)} %bitcast.3, s32[16,128]{1,0:T(8,128)} %bitcast.4, s32[16,128]{1,0:T(8,128)} %bitcast.5), custom_call_target="tpu_custom_call" | custom-call | tf_op jit(solution)/shard_map/pallas_call | solution.py:605
  55.7 0.6 %copy.6 = f32[8,1152]{1,0:T(8,128)} copy(f32[8,1152]{1,0:T(8,128)S(1)} %shard_map.46) | data formatting | bytes 73728
